TPU v7x, 768 devices: a whole 4x8x12 slice. The times are simulated.
768 devices in a mesh: inter: 16 (over x, z_lo), intra: 48 (over z_hi, y, core).
Axes of the slice: x: 4, y: 8, z: 12 (z_hi: 3, z_lo: 4; z = z_hi * 4 + z_lo), core: 2. Of those that a mesh axis runs over, the one named last changes fastest.
Arguments:
- layer_input: bfloat16 [98304, 4608], P(('inter', 'intra')), may hold values from -80 to 80
- norm_gain: bfloat16 [4608], P('intra'), may hold values from 0.5 to 1.5
- kv_weight: bfloat16 [4608, 128], P('intra'), may hold values from -0.09375 to 0.09375
- kv_cotangent: bfloat16 [98304, 128], P(('inter', 'intra')), may hold values from -24 to 24
Outputs:
- input_grad: bfloat16 [98304, 4608], P(('inter', 'intra'))
- weight_grad: float32 [4608, 128], P(('inter', 'intra'))
- gain_grad: float32 [4608], P(('inter', 'intra'))
All inputs are finite; a program needn't handle non-finite values.
Results may differ from a plain program's by a relative error of at most 0.0029.
Values may be sent and summed in bfloat16 or wider, within the bound.
No kernel may reach another device: no remote copies, remote signals or barrier semaphores. Data moves between devices by JAX's collectives and lax.ppermute only.
A program may use at most 64 MiB of HBM per device.

v0:
```python
import jax
import jax.numpy as jnp
from jax import lax
from jax.sharding import PartitionSpec as P

EPS = 1e-05


def in_one_piece(arrays, axis, dim, along):
    columns = [a.reshape(*a.shape[:along], -1) for a in arrays]
    both = jnp.concatenate(columns, axis=along)
    filled, at, gathered = (lax.all_gather(both, axis, axis=dim, tiled=True), 0, [])
    for a, column in zip(arrays, columns):
        slab = filled[..., at : at + column.shape[along]]
        gathered.append(slab.reshape(*slab.shape[:along], *a.shape[along:]))
        at += column.shape[along]
    return tuple(gathered)


def side_by_side(arrays, axis, dim, along):
    columns = [a.reshape(*a.shape[:along], -1) for a in arrays]
    both = jnp.concatenate(columns, axis=along)
    filled, at, gathered = (lax.psum_scatter(both, axis, scatter_dimension=dim, tiled=True), 0, [])
    for a, column in zip(arrays, columns):
        slab = filled[..., at : at + column.shape[along]]
        gathered.append(slab.reshape(*slab.shape[:along], *a.shape[along:]))
        at += column.shape[along]
    return tuple(gathered)


def in_blocks(x, dim, peers):
    lengths = x.shape
    pieces = x.reshape(*lengths[:dim], peers, lengths[dim] // peers, *lengths[dim + 1 :])
    return jnp.moveaxis(pieces, dim, 0)


def sent_and_summed(x, axis, dim):
    pieces = in_blocks(x, dim, lax.axis_size(axis))
    arrived = lax.all_to_all(pieces, axis, split_axis=0, concat_axis=0, tiled=True)
    return arrived.sum(axis=0)


def side_by_side_2(arrays, axis, dim, along):
    columns = [a.reshape(*a.shape[:along], -1) for a in arrays]
    both = jnp.concatenate(columns, axis=along)
    filled, at, gathered = (sent_and_summed(both, axis, dim), 0, [])
    for a, column in zip(arrays, columns):
        slab = filled[..., at : at + column.shape[along]]
        gathered.append(slab.reshape(*slab.shape[:along], *a.shape[along:]))
        at += column.shape[along]
    return tuple(gathered)


def on_device(layer_input, norm_gain, kv_weight, kv_cotangent):
    weight_all, gain_all = in_one_piece((kv_weight, norm_gain), "intra", 0, 1)
    gain_wide = gain_all.astype(jnp.float32)
    widened = layer_input.astype(jnp.float32)
    inverse_rms = lax.rsqrt(jnp.mean(widened * widened, axis=1, keepdims=True) + EPS)
    normal_rows = widened * inverse_rms
    normed = (normal_rows * gain_wide).astype(jnp.bfloat16)
    weight_term = lax.dot_general(
        normed, kv_cotangent, (((0,), (0,)), ((), ())), preferred_element_type=jnp.float32
    )
    feature_grad = lax.dot_general(
        kv_cotangent, weight_all, (((1,), (1,)), ((), ())), preferred_element_type=jnp.float32
    )
    gain_term = jnp.sum(feature_grad * normal_rows, axis=0)
    outer_count = lax.axis_size("inter")
    inner_count = lax.axis_size("intra")
    devices = outer_count * inner_count
    part_weight, part_gain = side_by_side((weight_term, gain_term), "inter", 0, 1)
    weight_grad, gain_grad = side_by_side_2((part_weight, part_gain), "intra", 0, 1)
    scaled_grad = feature_grad * gain_wide
    centre = jnp.mean(scaled_grad * normal_rows, axis=1, keepdims=True)
    input_grad = (inverse_rms * (scaled_grad - normal_rows * centre)).astype(jnp.bfloat16)
    return (input_grad, weight_grad / float(devices), gain_grad / float(devices))


def solution(mesh):
    return jax.shard_map(
        on_device,
        mesh=mesh,
        in_specs=(
            P(("inter", "intra"), None),
            P("intra"),
            P("intra", None),
            P(("inter", "intra"), None),
        ),
        out_specs=(P(("inter", "intra"), None), P(("inter", "intra"), None), P(("inter", "intra"))),
        check_vma=False,
    )
```

profile of v0, /device:TPU:1, one launch (start us, length us, event | category | flops | bytes accessed | tf_op | source)
XLA Modules:
  0.0 291.5 jit_solution(9308337714885489514)
XLA Ops:
  7.2 0.0 copy-start
  7.2 0.0 all-gather.3.cloned.1.call-start
  7.2 0.8 copy.20
  8.1 1.3 maximum_bitcast_fusion
  9.4 0.0 all-gather.3.cloned.1.call-update
  9.4 0.0 reduce-scatter.4.cloned.1.call-start
  9.4 1.7 copy.19
  11.1 0.6 fusion.10
  11.8 108.8 %all-gather.3.cloned.1.call-done = bf16[48,96,129]{1,2,0:T(8,128)(2,1)} async-done(((bf16[1,96,129]{1,2,0:T(8,128)(2,1)}), bf16[48,96,129]{1,2,0:T(8,128)(2,1)}) %all-gather.3.cloned.1.call-update) | async-done | bytes 1188880 | tf_op jit(solution)/shard_map/all_gather | solution.py:12
  120.6 1.6 copy.21
  122.3 3.0 %reshape.43 = bf16[4608,129]{0,1:T(8,128)(2,1)} reshape(bf16[48,96,129]{1,0,2:T(8,128)(2,1)S(1)} %copy.21) | data formatting | bytes 2377728
  125.2 0.9 fusion.16
  126.2 0.0 copy-done
  126.2 4.3 %fusion.9 = (f32[4608]{0:T(1024)S(1)}, f32[128]{0:T(128)S(1)}, f32[128,4608]{0,1:T(8,128)}) fusion(bf16[128,4608]{0,1:T(8,128)(2,1)S(1)} %copy.19, f32[128]{0:T(128)S(1)} %add_rsqrt_fusion, f32[4608]{0:T(1024)S(1)} %fusion.16, bf16[128,128]{1,0:T(8,128)(2,1)S(1)} %copy-done, bf16[4608,129]{0,1:T(8,128)(2,1)} %reshape.43), kind=kOutput, calls=%fused_computation.13 | convolution fusion | flops 155118976 | bytes 4789248 | tf_op jit(solution)/shard_map/dot_general | solution.py:64
  130.5 0.9 fusion.11
  131.5 1.7 pad_maximum_fusion
  133.2 5.0 %copy.24 = f32[4608,129]{1,0:T(8,128)} copy(f32[4608,129]{0,1:T(8,128)} %pad_maximum_fusion) | data formatting | bytes 4755456
  138.1 0.0 reduce-scatter.4.cloned.1.call-update
  138.2 114.2 %reduce-scatter.4.cloned.1.call-done = f32[288,129]{1,0:T(8,128)} async-done(((f32[4608,129]{1,0:T(8,128)}), f32[288,129]{1,0:T(8,128)}) %reduce-scatter.4.cloned.1.call-update) | async-done | bytes 148624 | tf_op jit(solution)/shard_map/reduce_scatter | solution.py:23
  252.4 1.0 reshape.40
  253.4 1.0 reshape.48
  254.4 13.2 %all-to-all-start = ((f32[48,1,774]{2,1,0:T(1,128)}), f32[48,1,774]{2,1,0:T(1,128)S(1)}, u32[]{:S(2)}, u32[]{:S(2)}) async-start(f32[48,1,774]{2,1,0:T(1,128)} %reshape.48), calls=%async_computation | async-start | bytes 344064 | tf_op jit(solution)/shard_map/all_to_all | solution.py:39
  267.6 3.2 %fusion.7 = bf16[128,4608]{0,1:T(8,128)(2,1)S(1)} fusion(bf16[128,4608]{0,1:T(8,128)(2,1)S(1)} %copy.19, f32[128,4608]{0,1:T(8,128)} %get-tuple-element.17, f32[128]{0:T(128)S(1)} %broadcast_multiply_fusion, f32[4608]{0:T(1024)S(1)} %fusion.16, f32[128]{0:T(128)S(1)} %add_rsqrt_fusion), kind=kLoop, calls=%fused_computation.11 | loop fusion | flops 4128768 | bytes 4738048 | tf_op jit(solution)/shard_map/convert_element_type | solution.py:75
  270.9 1.4 copy.23
  272.3 9.3 %all-to-all-done = f32[48,1,774]{2,1,0:T(1,128)S(1)} async-done(((f32[48,1,774]{2,1,0:T(1,128)}), f32[48,1,774]{2,1,0:T(1,128)S(1)}, u32[]{:S(2)}, u32[]{:S(2)}) %all-to-all-start) | async-done | bytes 148640 | tf_op jit(solution)/shard_map/all_to_all | solution.py:39
  281.6 0.5 broadcast.34
  282.1 1.0 reduce.4
  283.1 0.2 reshape.49
  283.3 0.1 reduce_sum.39
  283.4 0.6 slice_multiply_fusion.1
  284.0 0.6 fusion.17
  (3 shorter events, 0.0 us)
Async XLA Ops:
  7.2 119.0 %copy-start = (bf16[128,128]{1,0:T(8,128)(2,1)S(1)}, bf16[128,128]{1,0:T(8,128)(2,1)}, u32[]{:S(2)}) copy-start(bf16[128,128]{1,0:T(8,128)(2,1)} %param.7) | copy-start | bytes 98308
  7.2 113.4 %all-gather.3.cloned.1.call-start = ((), (), s32[]{:S(2)}) async-start(), calls=%async_computation.2 | async-start | bytes 1705984 | tf_op jit(solution)/shard_map/all_gather | solution.py:12
  9.4 243.0 %reduce-scatter.4.cloned.1.call-start = ((), (), s32[]{:S(2)}) async-start(), calls=%async_computation.3 | async-start | bytes 5013504 | tf_op jit(solution)/shard_map/reduce_scatter | solution.py:23
  254.4 27.1 %all-to-all-start = ((f32[48,1,774]{2,1,0:T(1,128)}), f32[48,1,774]{2,1,0:T(1,128)S(1)}, u32[]{:S(2)}, u32[]{:S(2)}) async-start(f32[48,1,774]{2,1,0:T(1,128)} %reshape.48), calls=%async_computation | async-start | bytes 344064 | tf_op jit(solution)/shard_map/all_to_all | solution.py:39
Sparse Core Ops, SparseCore 0:
  12.5 108.0 all-gather.2
  138.3 114.0 reduce-scatter.3
where the time goes:
time: 292 us; the launch traced here: 291 us
  waiting for transfers between devices  232 us (79%)
  local copies, waits for them, and re-layouts  16.3 us (6%)
  between operations  14.1 us (5%)
  starting transfers between devices  13.3 us (5%)
  other arithmetic  10.1 us (3%)
  matrix products  5.29 us (2%)
    reduce_scatter x1, waiting for transfers between devices, side_by_side(): lax.psum_scatter(both, axis, scatter_dimension=dim, tiled=True)  114 us
    all_gather x1, waiting for transfers between devices, in_one_piece(): lax.all_gather(both, axis, axis=dim, tiled=True)  109 us
    all_to_all x1, starting transfers between devices, sent_and_summed(): lax.all_to_all(pieces, axis, split_axis=0, concat_axis=0, tiled=True)  13.2 us
    unnamed x9, local copies, waits for them, and re-layouts  13.1 us
    all_to_all x1, waiting for transfers between devices, sent_and_summed(): lax.all_to_all(pieces, axis, split_axis=0, concat_axis=0, tiled=True)  9.25 us
  transfers between devices with their start and end apart: 3, of which 3 were waited for; matrix products, arithmetic and copies ran while one was open for 2% of the time, Pallas kernels for 0%

commit v1 on v0

v1 whole, which is shorter than its diff:
```python
import jax
import jax.numpy as jnp
from jax import lax
from jax.experimental import pallas as pl
from jax.experimental.pallas import tpu as pltpu
from jax.sharding import Mesh, PartitionSpec as P

EPS = 1e-05
X, ZL, ZH, Y, C = 4, 4, 3, 8, 2
INTER, PEERS = X * ZL, ZH * Y
DEVICES = INTER * PEERS * C
TOK, D, H = 128, 4608, 128
ROWS = D // DEVICES
SHARD = D // (PEERS * C)
SLAB = SHARD + 16
HALF = D // C
PART = HALF // INTER
CHUNK = 512
BF16, F16, F32 = jnp.bfloat16, jnp.float16, jnp.float32
VMEM = pl.BlockSpec(memory_space=pltpu.VMEM)
MIB = 1024 * 1024


def row_terms(x_ref, far_ref, cot_ref, far_cot_ref, half_ref, inv_ref, all_ref):
    def inverse(ref):
        square = jnp.zeros((TOK, 128), F32)
        for at in range(0, D, 128):
            wide = ref[:, at : at + 128].astype(F32)
            square += wide * wide
        return lax.rsqrt(jnp.sum(square, axis=1, keepdims=True) * (1.0 / D) + EPS)

    inv = inverse(x_ref)
    inv_ref[...] = jnp.broadcast_to(inv, (TOK, 128))
    near, far = cot_ref[...].astype(F32), far_cot_ref[...].astype(F32)
    largest = jnp.max(jnp.maximum(jnp.abs(near), jnp.abs(far)), axis=(0, 1), keepdims=True)
    power = jnp.ceil(jnp.log2(jnp.maximum(largest, 1e-30)))
    scale = jnp.exp2(-power)
    scaled = jnp.concatenate([near * (inv * scale), far * (inverse(far_ref) * scale)], axis=0)
    high = scaled.astype(BF16)
    low = (scaled - high.astype(F32)).astype(BF16)
    both = jnp.concatenate([high, low], axis=1)
    for at in range(0, D, CHUNK):
        turned = jnp.concatenate([x_ref[:, at : at + CHUNK].T, far_ref[:, at : at + CHUNK].T], axis=1)
        pair = jnp.dot(turned, both, preferred_element_type=F32)
        all_ref[at : at + CHUNK, :] = pair[:, :H] + pair[:, H:]
    mine = lax.axis_index("core")
    for group in range(INTER):
        for row in range(ROWS):
            start = group * C * PART + row
            to = slice(row * PEERS, (row + 1) * PEERS)
            half_ref[group, to, :] = all_ref[pl.ds(start + mine * ROWS, PEERS, stride=C * ROWS), :]
        half_ref[group, PART:, :] = jnp.broadcast_to(power, (8, H))


def group_sum(parts_ref, out_ref, sum_ref):
    total = jnp.zeros((PART, H), F32)
    for group in range(INTER):
        total += parts_ref[group, :PART] * jnp.exp2(parts_ref[group, PART : PART + 1, :])
    sum_ref[:PART, :] = total
    sum_ref[PART:, :] = jnp.zeros((8 * PEERS - PART, H), F32)
    for peer in range(PEERS):
        out_ref[peer] = sum_ref[pl.ds(peer, 8, stride=PEERS), :]


def input_side(x_ref, cot_ref, inv_ref, own_ref, other_ref, grad_ref, rows_ref, gains_ref, w_ref, g_ref, sg_ref, win_ref):
    mine, my_y, my_zh = lax.axis_index("core"), lax.axis_index("y"), lax.axis_index("zh")
    for hop in range(Y // 2):
        base_y = lax.rem(my_y + Y - 2 * hop, Y)
        for side in range(2):
            from_y = base_y if side == 0 else base_y + 1 - 2 * lax.rem(base_y, 2)
            for turn in range(ZH):
                peer = lax.rem(my_zh + ZH - turn, ZH) * Y + from_y
                for ref, core in ((own_ref, mine), (other_ref, 1 - mine)):
                    shard = 2 * peer + core
                    w_ref[pl.ds(pl.multiple_of(shard * SHARD, SHARD), SHARD), :] = ref[hop, side, turn, :SHARD, :]
                    g_ref[lax.rem(shard, 4), pl.ds(shard // 4, 1), :] = ref[hop, side, turn, SHARD:, :].astype(F32)[:1]
    w_ref[D:, :] = jnp.zeros((32, H), BF16)
    lane = lax.broadcasted_iota(jnp.int32, (16, 128), 1)
    g0, g1, g2, g3 = g_ref[0], g_ref[1], g_ref[2], g_ref[3]
    tiles = (
        jnp.where(lane < 96, g0, pltpu.roll(g1, 96, 1)),
        jnp.where(lane < 64, pltpu.roll(g1, 96, 1), pltpu.roll(g2, 64, 1)),
        jnp.where(lane < 32, pltpu.roll(g2, 64, 1), pltpu.roll(g3, 32, 1)),
    )
    first = ((lax.axis_index("x") * ZL + lax.axis_index("zl")) * PEERS + my_zh * Y + my_y) * C
    first = (first + mine) * ROWS
    base = pl.multiple_of(first // 16 * 16, 16)
    win_ref[:32, :] = w_ref[pl.ds(base, 32), :].astype(F32)
    rows_ref[...] = win_ref[pl.ds(first - base, 8), :]
    wanted = first + lax.broadcasted_iota(jnp.int32, (8, 128), 0)
    column = lax.broadcasted_iota(jnp.int32, (8, 128), 1)
    found = jnp.zeros((8, 128), F32)
    centre = jnp.zeros((TOK, 128), F32)
    inv = inv_ref[...]
    cot = cot_ref[...]
    for at in range(0, D, CHUNK):
        grad = lax.dot_general(cot, w_ref[at : at + CHUNK, :], (((1,), (1,)), ((), ())), preferred_element_type=F32)
        for tile in range(CHUNK // 128):
            here = at + tile * 128
            number = here // 128
            gain = tiles[number % 3][number // 3 : number // 3 + 1, :]
            found += jnp.where(column + here == wanted, gain, 0.0)
            scaled = grad[:, tile * 128 : tile * 128 + 128] * gain
            sg_ref[:, here : here + 128] = scaled
            centre += scaled * (x_ref[:, here : here + 128].astype(F32) * inv)
    gains_ref[...] = jnp.broadcast_to(jnp.sum(found, axis=1, keepdims=True), (8, 128))
    mean = jnp.broadcast_to(jnp.sum(centre, axis=1, keepdims=True) * (1.0 / D), (TOK, 128))
    for here in range(0, D, 128):
        normal = x_ref[:, here : here + 128].astype(F32) * inv
        grad_ref[:, here : here + 128] = (inv * (sg_ref[:, here : here + 128] - normal * mean)).astype(BF16)


def last_sum(parts_ref, rows_ref, gains_ref, weight_ref, gain_ref):
    total = parts_ref[0]
    for peer in range(1, PEERS):
        total += parts_ref[peer]
    total = total * (1.0 / DEVICES)
    weight_ref[...] = (total * gains_ref[...])[:ROWS]
    gain_ref[...] = jnp.broadcast_to(jnp.sum(total * rows_ref[...], axis=1, keepdims=True), (8, 128))


def call(body, outs, scratch=(), flops=0, moved=0):
    return pl.pallas_call(
        body,
        out_shape=[jax.ShapeDtypeStruct(*o) for o in outs],
        scratch_shapes=list(scratch),
        compiler_params=pltpu.CompilerParams(vmem_limit_bytes=40 * MIB),
        cost_estimate=pl.CostEstimate(flops=flops, bytes_accessed=moved, transcendentals=0),
    )


def swap_cores(a):
    return lax.ppermute(a, "core", [(0, 1), (1, 0)])


def shift(a, axis, n, by):
    return lax.ppermute(a, axis, [(i, (i + by) % n) for i in range(n)])


def gathered(slab):
    column = jnp.stack([slab] + [shift(slab, "zh", ZH, turn) for turn in range(1, ZH)])
    two = jnp.stack([column, lax.ppermute(column, "y", [(i, i ^ 1) for i in range(Y)])])
    return jnp.stack([two] + [shift(two, "y", Y, 2 * hop) for hop in range(1, Y // 2)])


def on_device(layer_input, norm_gain, kv_weight, kv_cotangent):
    far, far_cot = swap_cores(layer_input), swap_cores(kv_cotangent)
    gains = jnp.broadcast_to(jnp.pad(norm_gain, (0, 128 - SHARD))[None], (16, 128))
    own = gathered(jnp.concatenate([kv_weight, gains], axis=0))
    other = swap_cores(own)

    half, inv = call(
        row_terms,
        [((INTER, PART + 8, H), F32), ((TOK, 128), F32)],
        [pltpu.VMEM((D, H), F32)],
        flops=4 * TOK * D * H * 2,
        moved=4 * TOK * D + 2 * D * H,
    )(layer_input, far, kv_cotangent, far_cot)
    parts = lax.all_to_all(half.astype(F16), ("x", "zl"), split_axis=0, concat_axis=0, tiled=True).astype(F32)
    (sums,) = call(group_sum, [((PEERS, 8, H), F32)], [pltpu.VMEM((8 * PEERS, H), F32)], flops=INTER * PART * H, moved=4 * HALF * H)(parts)
    last = lax.all_to_all(sums, ("zh", "y"), split_axis=0, concat_axis=0, tiled=True)

    input_grad, rows, row_gains = call(
        input_side,
        [((TOK, D), BF16), ((8, H), F32), ((8, H), F32)],
        [
            pltpu.VMEM((D + 32, H), BF16),
            pltpu.VMEM((4, 16, 128), F32),
            pltpu.VMEM((TOK, D), F32),
            pltpu.VMEM((32 + 8, H), F32),
        ],
        flops=2 * TOK * D * H,
        moved=4 * TOK * D,
    )(layer_input, kv_cotangent, inv, own, other)
    weight_grad, gain_grad = call(last_sum, [((ROWS, H), F32), ((8, 128), F32)], flops=PEERS * 1024, moved=PEERS * 4096)(
        last, rows, row_gains
    )
    return input_grad, weight_grad, gain_grad[:ROWS, 0]


def solution(mesh):
    axes = ("x", "zl", "zh", "y", "core")
    fine = Mesh(mesh.devices.reshape(X, ZL, ZH, Y, C), axes)
    intra = ("zh", "y", "core")
    return jax.shard_map(
        on_device,
        mesh=fine,
        in_specs=(P(axes, None), P(intra), P(intra, None), P(axes, None)),
        out_specs=(P(axes, None), P(axes, None), P(axes)),
        check_vma=False,
    )
```

time: 292 us -> 103 us (0.35)
  the two profiles are of different devices: /device:TPU:1 before, /device:TPU:66 now
where the time goes in v1:
time: 103 us; the launch traced here: 102 us
  starting transfers between devices  58.4 us (57%)
  waiting for transfers between devices  34.1 us (33%)
  Pallas kernels  5.34 us (5%)
  local copies, waits for them, and re-layouts  2.69 us (3%)
  other arithmetic  1.13 us (1%)
    ppermute x5, starting transfers between devices, shift(): return lax.ppermute(a, axis, [(i, (i + by) % n) for i in range(n)])  25.6 us
    ppermute x5, waiting for transfers between devices, shift(): return lax.ppermute(a, axis, [(i, (i + by) % n) for i in range(n)])  20.1 us
    all_to_all x1, starting transfers between devices, on_device(): lax.all_to_all(half.astype(F16), ('x', 'zl'), split_axis=0, concat_axis=0...  12 us
    all_to_all x1, starting transfers between devices, on_device(): lax.all_to_all(sums, ('zh', 'y'), split_axis=0, concat_axis=0, tiled=True)  11 us
    all_to_all x1, waiting for transfers between devices, on_device(): lax.all_to_all(sums, ('zh', 'y'), split_axis=0, concat_axis=0, tiled=True)  10 us
    ppermute x3, starting transfers between devices, swap_cores(): return lax.ppermute(a, 'core', [(0, 1), (1, 0)])  6.25 us
    ppermute x1, starting transfers between devices, gathered(): lax.ppermute(column, 'y', [(i, i ^ 1) for i in range(Y)])  3.49 us
    ppermute x1, waiting for transfers between devices, gathered(): lax.ppermute(column, 'y', [(i, i ^ 1) for i in range(Y)])  2.89 us
  transfers between devices with their start and end apart: 11, of which 7 were waited for; matrix products, arithmetic and copies ran while one was open for 0% of the time, Pallas kernels for 3%

profile of v1, /device:TPU:66, one launch (start us, length us, event | category | flops | bytes accessed | tf_op | source)
XLA Modules:
  0.0 102.5 jit_solution(10376149815845760965)
XLA Ops:
  0.6 1.9 %collective-permute-start = (bf16[128,4608]{1,0:T(8,128)(2,1)}, bf16[128,4608]{1,0:T(8,128)(2,1)S(1)}, u32[]{:S(2)}, u32[]{:S(2)}) collective-permute-start(bf16[128,4608]{1,0:T(8,128)(2,1)} %x_ref.3), channel_id=1, source_target_pairs={{0,1},{1,0},{2,3},{3,2},{4,5},{5,4},{6,7},{7,6},{8,9},{9,8},{10,11... | collective-permute-start | bytes 3538952 | tf_op jit(solution)/shard_map/ppermute | solution.py:133
  2.6 2.4 %collective-permute-start.1 = (bf16[128,128]{1,0:T(8,128)(2,1)}, bf16[128,128]{1,0:T(8,128)(2,1)S(1)}, u32[]{:S(2)}, u32[]{:S(2)}) collective-permute-start(bf16[128,128]{1,0:T(8,128)(2,1)} %cot_ref.3), channel_id=1, source_target_pairs={{0,1},{1,0},{2,3},{3,2},{4,5},{5,4},{6,7},{7,6},{8,9},{9,8},{10,11... | collective-permute-start | bytes 98312 | tf_op jit(solution)/shard_map/ppermute | solution.py:133
  5.0 1.0 %collective-permute-done.1.far_cot_ref = bf16[128,128]{1,0:T(8,128)(2,1)S(1)} collective-permute-done((bf16[128,128]{1,0:T(8,128)(2,1)}, bf16[128,128]{1,0:T(8,128)(2,1)S(1)}, u32[]{:S(2)}, u32[]{:S(2)}) %collective-permute-start.1) | collective-permute-done | bytes 32800 | tf_op jit(solution)/shard_map/ppermute | solution.py:133
  6.0 0.0 collective-permute-done.far_ref
  6.0 0.0 copy-start
  6.0 1.3 %copy-done = bf16[128,4608]{1,0:T(8,128)(2,1)S(1)} copy-done((bf16[128,4608]{1,0:T(8,128)(2,1)S(1)}, bf16[128,4608]{1,0:T(8,128)(2,1)}, u32[]{:S(2)}) %copy-start) | copy-done | bytes 1179672
  7.3 0.0 copy-start.2
  7.3 0.8 copy-done.2
  8.1 1.4 %shard_map.67 = (f32[16,152,128]{2,1,0:T(8,128)S(1)}, f32[128,128]{1,0:T(8,128)S(1)}) custom-call(bf16[128,4608]{1,0:T(8,128)(2,1)S(1)} %copy-done, bf16[128,4608]{1,0:T(8,128)(2,1)S(1)} %collective-permute-done.far_ref, bf16[128,128]{1,0:T(8,128)(2,1)S(1)} %copy-done.2, bf16[128,128]{1,0:T(8,128)(2,1)S(1)} %collective-permute-done.1.far_cot_ref), custom_call_target="tpu_custom_call" | custom-call | flops 603979776 | bytes 3538944 | tf_op jit(solution)/shard_map/pallas_call | solution.py:152
  9.4 0.0 copy-start.5
  9.4 0.0 copy-start.4
  9.4 0.9 convert_element_type.8
  10.4 12.0 %all-to-all-start = ((f16[16,152,128]{2,1,0:T(8,128)(2,1)}), f16[16,152,128]{2,1,0:T(8,128)(2,1)S(1)}, u32[]{:S(2)}, u32[]{:S(2)}) async-start(f16[16,152,128]{2,1,0:T(8,128)(2,1)} %convert_element_type.8), calls=%async_computation | async-start | bytes 1245184 | tf_op jit(solution)/shard_map/all_to_all | solution.py:159
  22.4 0.0 copy-done.5
  22.4 0.0 copy-done.4
  22.4 9.2 %collective-permute-start.3 = (bf16[112,128]{1,0:T(8,128)(2,1)S(1)}, bf16[112,128]{1,0:T(8,128)(2,1)S(1)}, u32[]{:S(2)}, u32[]{:S(2)}) collective-permute-start(bf16[112,128]{1,0:T(8,128)(2,1)S(1)} %get-tuple-element.22), channel_id=1, source_target_pairs={{0,32},{16,0},{32,16},{1,33},{17,1},{33,17},{2,34},{18,2},{34,18},... | collective-permute-start | bytes 86024 | tf_op jit(solution)/shard_map/ppermute | solution.py:137
  31.6 1.9 %collective-permute-start.2 = (bf16[112,128]{1,0:T(8,128)(2,1)S(1)}, bf16[112,128]{1,0:T(8,128)(2,1)S(1)}, u32[]{:S(2)}, u32[]{:S(2)}) collective-permute-start(bf16[112,128]{1,0:T(8,128)(2,1)S(1)} %get-tuple-element.22), channel_id=1, source_target_pairs={{0,16},{16,32},{32,0},{1,17},{17,33},{33,1},{2,18},{18,34},{34,2},... | collective-permute-start | bytes 86024 | tf_op jit(solution)/shard_map/ppermute | solution.py:137
  33.6 3.7 %collective-permute-done.3 = bf16[112,128]{1,0:T(8,128)(2,1)S(1)} collective-permute-done((bf16[112,128]{1,0:T(8,128)(2,1)S(1)}, bf16[112,128]{1,0:T(8,128)(2,1)S(1)}, u32[]{:S(2)}, u32[]{:S(2)}) %collective-permute-start.3) | collective-permute-done | bytes 28704 | tf_op jit(solution)/shard_map/ppermute | solution.py:137
  37.3 9.0 %collective-permute-done.2 = bf16[112,128]{1,0:T(8,128)(2,1)S(1)} collective-permute-done((bf16[112,128]{1,0:T(8,128)(2,1)S(1)}, bf16[112,128]{1,0:T(8,128)(2,1)S(1)}, u32[]{:S(2)}, u32[]{:S(2)}) %collective-permute-start.2) | collective-permute-done | bytes 28704 | tf_op jit(solution)/shard_map/ppermute | solution.py:137
  46.4 3.5 %collective-permute-start.4 = (bf16[3,112,128]{2,1,0:T(8,128)(2,1)S(1)}, bf16[3,112,128]{2,1,0:T(8,128)(2,1)S(1)}, u32[]{:S(2)}, u32[]{:S(2)}) collective-permute-start(bf16[3,112,128]{2,1,0:T(8,128)(2,1)S(1)} %get-tuple-element.20), channel_id=1, source_target_pairs={{0,2},{2,0},{4,6},{6,4},{8,10},{10,8},{12,14},{14,12},{1,3},{3,1},... | collective-permute-start | bytes 258056 | tf_op jit(solution)/shard_map/ppermute | solution.py:142
  49.9 2.9 %collective-permute-done.4 = bf16[3,112,128]{2,1,0:T(8,128)(2,1)S(1)} collective-permute-done((bf16[3,112,128]{2,1,0:T(8,128)(2,1)S(1)}, bf16[3,112,128]{2,1,0:T(8,128)(2,1)S(1)}, u32[]{:S(2)}, u32[]{:S(2)}) %collective-permute-start.4) | collective-permute-done | bytes 86048 | tf_op jit(solution)/shard_map/ppermute | solution.py:142
  52.8 6.2 %collective-permute-start.7 = (bf16[2,3,112,128]{3,2,1,0:T(8,128)(2,1)S(1)}, bf16[2,3,112,128]{3,2,1,0:T(8,128)(2,1)S(1)}, u32[]{:S(2)}, u32[]{:S(2)}) collective-permute-start(bf16[2,3,112,128]{3,2,1,0:T(8,128)(2,1)S(1)} %get-tuple-element.18), channel_id=1, source_target_pairs={{0,12},{2,14},{4,0},{6,2},{8,4},{10,6},{12,8},{14,10},{1,13},{3,15... | collective-permute-start | bytes 516104 | tf_op jit(solution)/shard_map/ppermute | solution.py:137
  59.0 3.8 %collective-permute-start.6 = (bf16[2,3,112,128]{3,2,1,0:T(8,128)(2,1)S(1)}, bf16[2,3,112,128]{3,2,1,0:T(8,128)(2,1)S(1)}, u32[]{:S(2)}, u32[]{:S(2)}) collective-permute-start(bf16[2,3,112,128]{3,2,1,0:T(8,128)(2,1)S(1)} %get-tuple-element.18), channel_id=1, source_target_pairs={{0,8},{2,10},{4,12},{6,14},{8,0},{10,2},{12,4},{14,6},{1,9},{3,11}... | collective-permute-start | bytes 516104 | tf_op jit(solution)/shard_map/ppermute | solution.py:137
  62.8 4.5 %collective-permute-start.5 = (bf16[2,3,112,128]{3,2,1,0:T(8,128)(2,1)S(1)}, bf16[2,3,112,128]{3,2,1,0:T(8,128)(2,1)S(1)}, u32[]{:S(2)}, u32[]{:S(2)}) collective-permute-start(bf16[2,3,112,128]{3,2,1,0:T(8,128)(2,1)S(1)} %get-tuple-element.18), channel_id=1, source_target_pairs={{0,4},{2,6},{4,8},{6,10},{8,12},{10,14},{12,0},{14,2},{1,5},{3,7},... | collective-permute-start | bytes 516104 | tf_op jit(solution)/shard_map/ppermute | solution.py:137
  67.3 5.4 %collective-permute-done.7 = bf16[2,3,112,128]{3,2,1,0:T(8,128)(2,1)S(1)} collective-permute-done((bf16[2,3,112,128]{3,2,1,0:T(8,128)(2,1)S(1)}, bf16[2,3,112,128]{3,2,1,0:T(8,128)(2,1)S(1)}, u32[]{:S(2)}, u32[]{:S(2)}) %collective-permute-start.7) | collective-permute-done | bytes 172064 | tf_op jit(solution)/shard_map/ppermute | solution.py:137
  72.7 1.9 %collective-permute-done.6 = bf16[2,3,112,128]{3,2,1,0:T(8,128)(2,1)S(1)} collective-permute-done((bf16[2,3,112,128]{3,2,1,0:T(8,128)(2,1)S(1)}, bf16[2,3,112,128]{3,2,1,0:T(8,128)(2,1)S(1)}, u32[]{:S(2)}, u32[]{:S(2)}) %collective-permute-start.6) | collective-permute-done | bytes 172064 | tf_op jit(solution)/shard_map/ppermute | solution.py:137
  74.6 0.0 collective-permute-done.5
  74.6 0.1 pad_maximum_fusion.own_ref
  74.7 1.9 %collective-permute-start.8 = (bf16[4,2,3,112,128]{4,3,2,1,0:T(8,128)(2,1)S(1)}, bf16[4,2,3,112,128]{4,3,2,1,0:T(8,128)(2,1)S(1)}, u32[]{:S(2)}, u32[]{:S(2)}) collective-permute-start(bf16[4,2,3,112,128]{4,3,2,1,0:T(8,128)(2,1)S(1)} %pad_maximum_fusion.own_ref), channel_id=1, source_target_pairs={{0,1},{1,0},{2,3},{3,2},{4,5},{5,4},{6,7},{7,6},{8,9},{9,8},{10,11... | collective-permute-start | bytes 2064392 | tf_op jit(solution)/shard_map/ppermute | solution.py:133
  76.7 0.0 all-to-all-done
  76.7 0.1 convert_element_type.9.parts_ref
  76.8 0.0 copy-start.1
  76.8 0.0 copy-start.3
  76.8 0.8 shard_map.69
  77.5 11.0 %all-to-all-start.1 = ((f32[24,8,128]{2,1,0:T(8,128)}), f32[24,8,128]{2,1,0:T(8,128)S(1)}, u32[]{:S(2)}, u32[]{:S(2)}) async-start(f32[24,8,128]{2,1,0:T(8,128)} %shard_map.69), calls=%async_computation.1 | async-start | bytes 196608 | tf_op jit(solution)/shard_map/all_to_all | solution.py:161
  88.6 0.0 collective-permute-done.8.other_ref
  88.6 0.0 copy-done.1
  88.6 0.0 copy-done.3
  88.6 2.6 %shard_map.68 = (bf16[128,4608]{1,0:T(8,128)(2,1)}, f32[8,128]{1,0:T(8,128)S(1)}, f32[8,128]{1,0:T(8,128)S(1)}) custom-call(bf16[128,4608]{1,0:T(8,128)(2,1)S(1)} %copy-done.1, bf16[128,128]{1,0:T(8,128)(2,1)S(1)} %copy-done.3, f32[128,128]{1,0:T(8,128)S(1)} %get-tuple-element.10.inv_ref, bf16[4,2,3,112,128]{4,3,2,1,0:T(8,128)(2,1)S(1)} %pad_maximum_fusion.own_ref, ...), custom_call_target="tpu_custom_call" | custom-call | flops 150994944 | bytes 2359296 | tf_op jit(solution)/shard_map/pallas_call | solution.py:163
  91.2 10.0 %all-to-all-done.1.parts_ref = f32[24,8,128]{2,1,0:T(8,128)S(1)} async-done(((f32[24,8,128]{2,1,0:T(8,128)}), f32[24,8,128]{2,1,0:T(8,128)S(1)}, u32[]{:S(2)}, u32[]{:S(2)}) %all-to-all-start.1) | async-done | bytes 98336 | tf_op jit(solution)/shard_map/all_to_all | solution.py:161
  101.2 0.6 shard_map.70
  101.8 0.6 slice_reduce_fusion
  (5 shorter events, 0.1 us)
Async XLA Ops:
  0.6 5.4 %collective-permute-start = (bf16[128,4608]{1,0:T(8,128)(2,1)}, bf16[128,4608]{1,0:T(8,128)(2,1)S(1)}, u32[]{:S(2)}, u32[]{:S(2)}) collective-permute-start(bf16[128,4608]{1,0:T(8,128)(2,1)} %x_ref.3), channel_id=1, source_target_pairs={{0,1},{1,0},{2,3},{3,2},{4,5},{5,4},{6,7},{7,6},{8,9},{9,8},{10,11... | collective-permute-start | bytes 3538952 | tf_op jit(solution)/shard_map/ppermute | solution.py:133
  2.6 3.5 %collective-permute-start.1 = (bf16[128,128]{1,0:T(8,128)(2,1)}, bf16[128,128]{1,0:T(8,128)(2,1)S(1)}, u32[]{:S(2)}, u32[]{:S(2)}) collective-permute-start(bf16[128,128]{1,0:T(8,128)(2,1)} %cot_ref.3), channel_id=1, source_target_pairs={{0,1},{1,0},{2,3},{3,2},{4,5},{5,4},{6,7},{7,6},{8,9},{9,8},{10,11... | collective-permute-start | bytes 98312 | tf_op jit(solution)/shard_map/ppermute | solution.py:133
  6.0 1.3 %copy-start = (bf16[128,4608]{1,0:T(8,128)(2,1)S(1)}, bf16[128,4608]{1,0:T(8,128)(2,1)}, u32[]{:S(2)}) copy-start(bf16[128,4608]{1,0:T(8,128)(2,1)} %x_ref.3) | copy-start | bytes 3538948
  7.3 0.8 copy-start.2
  9.4 13.0 %copy-start.5 = (bf16[96]{0:T(256)(128)(2,1)S(1)}, bf16[96]{0:T(256)(128)(2,1)}, u32[]{:S(2)}) copy-start(bf16[96]{0:T(256)(128)(2,1)} %param.5) | copy-start | bytes 580
  9.4 13.0 %copy-start.4 = (bf16[96,128]{1,0:T(8,128)(2,1)S(1)}, bf16[96,128]{1,0:T(8,128)(2,1)}, u32[]{:S(2)}) copy-start(bf16[96,128]{1,0:T(8,128)(2,1)} %param.6) | copy-start | bytes 73732
  10.4 66.3 %all-to-all-start = ((f16[16,152,128]{2,1,0:T(8,128)(2,1)}), f16[16,152,128]{2,1,0:T(8,128)(2,1)S(1)}, u32[]{:S(2)}, u32[]{:S(2)}) async-start(f16[16,152,128]{2,1,0:T(8,128)(2,1)} %convert_element_type.8), calls=%async_computation | async-start | bytes 1245184 | tf_op jit(solution)/shard_map/all_to_all | solution.py:159
  22.4 14.9 %collective-permute-start.3 = (bf16[112,128]{1,0:T(8,128)(2,1)S(1)}, bf16[112,128]{1,0:T(8,128)(2,1)S(1)}, u32[]{:S(2)}, u32[]{:S(2)}) collective-permute-start(bf16[112,128]{1,0:T(8,128)(2,1)S(1)} %get-tuple-element.22), channel_id=1, source_target_pairs={{0,32},{16,0},{32,16},{1,33},{17,1},{33,17},{2,34},{18,2},{34,18},... | collective-permute-start | bytes 86024 | tf_op jit(solution)/shard_map/ppermute | solution.py:137
  31.6 14.7 %collective-permute-start.2 = (bf16[112,128]{1,0:T(8,128)(2,1)S(1)}, bf16[112,128]{1,0:T(8,128)(2,1)S(1)}, u32[]{:S(2)}, u32[]{:S(2)}) collective-permute-start(bf16[112,128]{1,0:T(8,128)(2,1)S(1)} %get-tuple-element.22), channel_id=1, source_target_pairs={{0,16},{16,32},{32,0},{1,17},{17,33},{33,1},{2,18},{18,34},{34,2},... | collective-permute-start | bytes 86024 | tf_op jit(solution)/shard_map/ppermute | solution.py:137
  46.4 6.4 %collective-permute-start.4 = (bf16[3,112,128]{2,1,0:T(8,128)(2,1)S(1)}, bf16[3,112,128]{2,1,0:T(8,128)(2,1)S(1)}, u32[]{:S(2)}, u32[]{:S(2)}) collective-permute-start(bf16[3,112,128]{2,1,0:T(8,128)(2,1)S(1)} %get-tuple-element.20), channel_id=1, source_target_pairs={{0,2},{2,0},{4,6},{6,4},{8,10},{10,8},{12,14},{14,12},{1,3},{3,1},... | collective-permute-start | bytes 258056 | tf_op jit(solution)/shard_map/ppermute | solution.py:142
  52.8 19.9 %collective-permute-start.7 = (bf16[2,3,112,128]{3,2,1,0:T(8,128)(2,1)S(1)}, bf16[2,3,112,128]{3,2,1,0:T(8,128)(2,1)S(1)}, u32[]{:S(2)}, u32[]{:S(2)}) collective-permute-start(bf16[2,3,112,128]{3,2,1,0:T(8,128)(2,1)S(1)} %get-tuple-element.18), channel_id=1, source_target_pairs={{0,12},{2,14},{4,0},{6,2},{8,4},{10,6},{12,8},{14,10},{1,13},{3,15... | collective-permute-start | bytes 516104 | tf_op jit(solution)/shard_map/ppermute | solution.py:137
  59.0 15.7 %collective-permute-start.6 = (bf16[2,3,112,128]{3,2,1,0:T(8,128)(2,1)S(1)}, bf16[2,3,112,128]{3,2,1,0:T(8,128)(2,1)S(1)}, u32[]{:S(2)}, u32[]{:S(2)}) collective-permute-start(bf16[2,3,112,128]{3,2,1,0:T(8,128)(2,1)S(1)} %get-tuple-element.18), channel_id=1, source_target_pairs={{0,8},{2,10},{4,12},{6,14},{8,0},{10,2},{12,4},{14,6},{1,9},{3,11}... | collective-permute-start | bytes 516104 | tf_op jit(solution)/shard_map/ppermute | solution.py:137
  62.8 11.9 %collective-permute-start.5 = (bf16[2,3,112,128]{3,2,1,0:T(8,128)(2,1)S(1)}, bf16[2,3,112,128]{3,2,1,0:T(8,128)(2,1)S(1)}, u32[]{:S(2)}, u32[]{:S(2)}) collective-permute-start(bf16[2,3,112,128]{3,2,1,0:T(8,128)(2,1)S(1)} %get-tuple-element.18), channel_id=1, source_target_pairs={{0,4},{2,6},{4,8},{6,10},{8,12},{10,14},{12,0},{14,2},{1,5},{3,7},... | collective-permute-start | bytes 516104 | tf_op jit(solution)/shard_map/ppermute | solution.py:137
  74.7 13.8 %collective-permute-start.8 = (bf16[4,2,3,112,128]{4,3,2,1,0:T(8,128)(2,1)S(1)}, bf16[4,2,3,112,128]{4,3,2,1,0:T(8,128)(2,1)S(1)}, u32[]{:S(2)}, u32[]{:S(2)}) collective-permute-start(bf16[4,2,3,112,128]{4,3,2,1,0:T(8,128)(2,1)S(1)} %pad_maximum_fusion.own_ref), channel_id=1, source_target_pairs={{0,1},{1,0},{2,3},{3,2},{4,5},{5,4},{6,7},{7,6},{8,9},{9,8},{10,11... | collective-permute-start | bytes 2064392 | tf_op jit(solution)/shard_map/ppermute | solution.py:133
  76.8 11.8 %copy-start.1 = (bf16[128,4608]{1,0:T(8,128)(2,1)S(1)}, bf16[128,4608]{1,0:T(8,128)(2,1)}, u32[]{:S(2)}) copy-start(bf16[128,4608]{1,0:T(8,128)(2,1)} %x_ref.3) | copy-start | bytes 3538948
  76.8 11.8 %copy-start.3 = (bf16[128,128]{1,0:T(8,128)(2,1)S(1)}, bf16[128,128]{1,0:T(8,128)(2,1)}, u32[]{:S(2)}) copy-start(bf16[128,128]{1,0:T(8,128)(2,1)} %cot_ref.3) | copy-start | bytes 98308
  77.5 23.7 %all-to-all-start.1 = ((f32[24,8,128]{2,1,0:T(8,128)}), f32[24,8,128]{2,1,0:T(8,128)S(1)}, u32[]{:S(2)}, u32[]{:S(2)}) async-start(f32[24,8,128]{2,1,0:T(8,128)} %shard_map.69), calls=%async_computation.1 | async-start | bytes 196608 | tf_op jit(solution)/shard_map/all_to_all | solution.py:161

commit v2 on v1

--- a/solution.py
+++ b/solution.py
@@ -21,34 +21,48 @@
 MIB = 1024 * 1024
 
 
-def row_terms(x_ref, far_ref, cot_ref, far_cot_ref, half_ref, inv_ref, all_ref):
-    def inverse(ref):
-        square = jnp.zeros((TOK, 128), F32)
-        for at in range(0, D, 128):
-            wide = ref[:, at : at + 128].astype(F32)
-            square += wide * wide
-        return lax.rsqrt(jnp.sum(square, axis=1, keepdims=True) * (1.0 / D) + EPS)
-
-    inv = inverse(x_ref)
-    inv_ref[...] = jnp.broadcast_to(inv, (TOK, 128))
-    near, far = cot_ref[...].astype(F32), far_cot_ref[...].astype(F32)
-    largest = jnp.max(jnp.maximum(jnp.abs(near), jnp.abs(far)), axis=(0, 1), keepdims=True)
-    power = jnp.ceil(jnp.log2(jnp.maximum(largest, 1e-30)))
-    scale = jnp.exp2(-power)
-    scaled = jnp.concatenate([near * (inv * scale), far * (inverse(far_ref) * scale)], axis=0)
+def inverse(ref):
+    square = jnp.zeros((TOK, 128), F32)
+    for at in range(0, D, 128):
+        wide = ref[:, at : at + 128].astype(F32)
+        square += wide * wide
+    return lax.rsqrt(jnp.sum(square, axis=1, keepdims=True) * (1.0 / D) + EPS)
+
+
+def products(x_ref, scaled, all_ref):
     high = scaled.astype(BF16)
     low = (scaled - high.astype(F32)).astype(BF16)
     both = jnp.concatenate([high, low], axis=1)
     for at in range(0, D, CHUNK):
-        turned = jnp.concatenate([x_ref[:, at : at + CHUNK].T, far_ref[:, at : at + CHUNK].T], axis=1)
-        pair = jnp.dot(turned, both, preferred_element_type=F32)
+        pair = jnp.dot(x_ref[:, at : at + CHUNK].T, both, preferred_element_type=F32)
         all_ref[at : at + CHUNK, :] = pair[:, :H] + pair[:, H:]
+
+
+def rows_of(all_ref, group, row, core):
+    return all_ref[pl.ds(group * C * PART + row + core * ROWS, PEERS, stride=C * ROWS), :]
+
+
+def near_terms(x_ref, cot_ref, half_ref, inv_ref, all_ref):
+    inv = inverse(x_ref)
+    inv_ref[...] = jnp.broadcast_to(inv, (TOK, 128))
+    products(x_ref, cot_ref[...].astype(F32) * inv, all_ref)
     mine = lax.axis_index("core")
     for group in range(INTER):
         for row in range(ROWS):
-            start = group * C * PART + row
+            half_ref[group, row * PEERS : (row + 1) * PEERS, :] = rows_of(all_ref, group, row, mine)
+
+
+def far_terms(x_ref, cot_ref, near_cot_ref, near_ref, half_ref, all_ref):
+    cot = cot_ref[...].astype(F32)
+    largest = jnp.max(jnp.maximum(jnp.abs(cot), jnp.abs(near_cot_ref[...].astype(F32))), axis=(0, 1), keepdims=True)
+    power = jnp.ceil(jnp.log2(jnp.maximum(largest, 1e-30)))
+    scale = jnp.exp2(-power)
+    products(x_ref, cot * (inverse(x_ref) * scale), all_ref)
+    mine = lax.axis_index("core")
+    for group in range(INTER):
+        for row in range(ROWS):
             to = slice(row * PEERS, (row + 1) * PEERS)
-            half_ref[group, to, :] = all_ref[pl.ds(start + mine * ROWS, PEERS, stride=C * ROWS), :]
+            half_ref[group, to, :] = rows_of(all_ref, group, row, mine) + near_ref[group, to, :] * scale
         half_ref[group, PART:, :] = jnp.broadcast_to(power, (8, H))
 
 
@@ -62,7 +76,7 @@
         out_ref[peer] = sum_ref[pl.ds(peer, 8, stride=PEERS), :]
 
 
-def input_side(x_ref, cot_ref, inv_ref, own_ref, other_ref, grad_ref, rows_ref, gains_ref, w_ref, g_ref, sg_ref, win_ref):
+def outputs(x_ref, cot_ref, inv_ref, own_ref, other_ref, total_ref, grad_ref, weight_ref, gain_ref, w_ref, g_ref, sg_ref, win_ref):
     mine, my_y, my_zh = lax.axis_index("core"), lax.axis_index("y"), lax.axis_index("zh")
     for hop in range(Y // 2):
         base_y = lax.rem(my_y + Y - 2 * hop, Y)
@@ -86,7 +100,6 @@
     first = (first + mine) * ROWS
     base = pl.multiple_of(first // 16 * 16, 16)
     win_ref[:32, :] = w_ref[pl.ds(base, 32), :].astype(F32)
-    rows_ref[...] = win_ref[pl.ds(first - base, 8), :]
     wanted = first + lax.broadcasted_iota(jnp.int32, (8, 128), 0)
     column = lax.broadcasted_iota(jnp.int32, (8, 128), 1)
     found = jnp.zeros((8, 128), F32)
@@ -103,20 +116,20 @@
             scaled = grad[:, tile * 128 : tile * 128 + 128] * gain
             sg_ref[:, here : here + 128] = scaled
             centre += scaled * (x_ref[:, here : here + 128].astype(F32) * inv)
-    gains_ref[...] = jnp.broadcast_to(jnp.sum(found, axis=1, keepdims=True), (8, 128))
+    total = total_ref[...]
+    weight_ref[...] = (total * jnp.sum(found, axis=1, keepdims=True))[:ROWS]
+    gain_ref[...] = jnp.sum((total * win_ref[pl.ds(first - base, 8), :]).T, axis=0)[:ROWS]
     mean = jnp.broadcast_to(jnp.sum(centre, axis=1, keepdims=True) * (1.0 / D), (TOK, 128))
     for here in range(0, D, 128):
         normal = x_ref[:, here : here + 128].astype(F32) * inv
         grad_ref[:, here : here + 128] = (inv * (sg_ref[:, here : here + 128] - normal * mean)).astype(BF16)
 
 
-def last_sum(parts_ref, rows_ref, gains_ref, weight_ref, gain_ref):
+def last_sum(parts_ref, total_ref):
     total = parts_ref[0]
     for peer in range(1, PEERS):
         total += parts_ref[peer]
-    total = total * (1.0 / DEVICES)
-    weight_ref[...] = (total * gains_ref[...])[:ROWS]
-    gain_ref[...] = jnp.broadcast_to(jnp.sum(total * rows_ref[...], axis=1, keepdims=True), (8, 128))
+    total_ref[...] = total * (1.0 / DEVICES)
 
 
 def call(body, outs, scratch=(), flops=0, moved=0):
@@ -137,32 +150,45 @@
     return lax.ppermute(a, axis, [(i, (i + by) % n) for i in range(n)])
 
 
-def gathered(slab):
-    column = jnp.stack([slab] + [shift(slab, "zh", ZH, turn) for turn in range(1, ZH)])
-    two = jnp.stack([column, lax.ppermute(column, "y", [(i, i ^ 1) for i in range(Y)])])
-    return jnp.stack([two] + [shift(two, "y", Y, 2 * hop) for hop in range(1, Y // 2)])
-
-
 def on_device(layer_input, norm_gain, kv_weight, kv_cotangent):
+    barrier = lax.optimization_barrier
     far, far_cot = swap_cores(layer_input), swap_cores(kv_cotangent)
     gains = jnp.broadcast_to(jnp.pad(norm_gain, (0, 128 - SHARD))[None], (16, 128))
-    own = gathered(jnp.concatenate([kv_weight, gains], axis=0))
-    other = swap_cores(own)
-
-    half, inv = call(
-        row_terms,
-        [((INTER, PART + 8, H), F32), ((TOK, 128), F32)],
+    slab = jnp.concatenate([kv_weight, gains], axis=0)
+    turns = [shift(slab, "zh", ZH, turn) for turn in range(1, ZH)]
+    near, inv = call(
+        near_terms,
+        [((INTER, PART, H), F32), ((TOK, 128), F32)],
         [pltpu.VMEM((D, H), F32)],
-        flops=4 * TOK * D * H * 2,
-        moved=4 * TOK * D + 2 * D * H,
-    )(layer_input, far, kv_cotangent, far_cot)
-    parts = lax.all_to_all(half.astype(F16), ("x", "zl"), split_axis=0, concat_axis=0, tiled=True).astype(F32)
+        flops=4 * TOK * D * H,
+        moved=2 * TOK * D + 2 * D * H,
+    )(layer_input, kv_cotangent)
+    turns, near = barrier((turns, near))
+    column = jnp.stack([slab] + turns)
+    beside = lax.ppermute(column, "y", [(i, i ^ 1) for i in range(Y)])
+    far, column = barrier((far, column))
+    (half,) = call(
+        far_terms,
+        [((INTER, PART + 8, H), F32)],
+        [pltpu.VMEM((D, H), F32)],
+        flops=4 * TOK * D * H,
+        moved=2 * TOK * D + 4 * D * H,
+    )(far, far_cot, kv_cotangent, near)
+    short = half.astype(F16)
+    beside, short = barrier((beside, short))
+    parts = lax.all_to_all(short, ("x", "zl"), split_axis=0, concat_axis=0, tiled=True).astype(F32)
+    two = jnp.stack([column, beside])
+    hops = [shift(two, "y", Y, 2 * hop) for hop in range(1, Y // 2)]
     (sums,) = call(group_sum, [((PEERS, 8, H), F32)], [pltpu.VMEM((8 * PEERS, H), F32)], flops=INTER * PART * H, moved=4 * HALF * H)(parts)
     last = lax.all_to_all(sums, ("zh", "y"), split_axis=0, concat_axis=0, tiled=True)
-
-    input_grad, rows, row_gains = call(
-        input_side,
-        [((TOK, D), BF16), ((8, H), F32), ((8, H), F32)],
+    hops, _ = barrier((hops, sums))
+    own = jnp.stack([two] + hops)
+    other = swap_cores(own)
+
+    (total,) = call(last_sum, [((8, H), F32)], flops=int(2e10), moved=PEERS * 4096)(last)
+    return call(
+        outputs,
+        [((TOK, D), BF16), ((ROWS, H), F32), ((ROWS,), F32)],
         [
             pltpu.VMEM((D + 32, H), BF16),
             pltpu.VMEM((4, 16, 128), F32),
@@ -171,11 +197,7 @@
         ],
         flops=2 * TOK * D * H,
         moved=4 * TOK * D,
-    )(layer_input, kv_cotangent, inv, own, other)
-    weight_grad, gain_grad = call(last_sum, [((ROWS, H), F32), ((8, 128), F32)], flops=PEERS * 1024, moved=PEERS * 4096)(
-        last, rows, row_gains
-    )
-    return input_grad, weight_grad, gain_grad[:ROWS, 0]
+    )(layer_input, kv_cotangent, inv, own, other, total)
 
 
 def solution(mesh):

time: 103 us -> 87.7 us (0.85)
  the two profiles are of different devices: /device:TPU:66 before, /device:TPU:8 now
where the time goes in v2:
time: 87.7 us; the launch traced here: 87 us
  starting transfers between devices  60.5 us (69%)
  waiting for transfers between devices  15.5 us (18%)
  Pallas kernels  5.57 us (6%)
  local copies, waits for them, and re-layouts  2.7 us (3%)
  other arithmetic  1.86 us (2%)
    ppermute x5, starting transfers between devices, shift(): return lax.ppermute(a, axis, [(i, (i + by) % n) for i in range(n)])  32.1 us
    all_to_all x1, starting transfers between devices, on_device(): lax.all_to_all(sums, ('zh', 'y'), split_axis=0, concat_axis=0, tiled=True)  11.2 us
    all_to_all x1, waiting for transfers between devices, on_device(): lax.all_to_all(sums, ('zh', 'y'), split_axis=0, concat_axis=0, tiled=True)  9.27 us
    all_to_all x1, starting transfers between devices, on_device(): lax.all_to_all(short, ('x', 'zl'), split_axis=0, concat_axis=0, tiled=True)  8.52 us
    ppermute x3, starting transfers between devices, swap_cores(): return lax.ppermute(a, 'core', [(0, 1), (1, 0)])  5.9 us
    all_to_all x1, waiting for transfers between devices, on_device(): lax.all_to_all(short, ('x', 'zl'), split_axis=0, concat_axis=0, tiled=True)  3.2 us
    ppermute x1, starting transfers between devices, on_device(): beside = lax.ppermute(column, 'y', [(i, i ^ 1) for i in range(Y)])  2.82 us
    pallas_call x1, Pallas kernels, on_device(): call(outputs, [((TOK, D), BF16), ((ROWS, H), F32), ((ROWS,), F32)], [pltp...  2.61 us
  transfers between devices with their start and end apart: 11, of which 4 were waited for; matrix products, arithmetic and copies ran while one was open for 3% of the time, Pallas kernels for 3%

profile of v2, /device:TPU:8, one launch (start us, length us, event | category | flops | bytes accessed | tf_op | source)
XLA Modules:
  0.0 87.0 jit_solution(10070267303511593695)
XLA Ops:
  0.6 1.9 %collective-permute-start = (bf16[128,4608]{1,0:T(8,128)(2,1)}, bf16[128,4608]{1,0:T(8,128)(2,1)S(1)}, u32[]{:S(2)}, u32[]{:S(2)}) collective-permute-start(bf16[128,4608]{1,0:T(8,128)(2,1)} %x_ref.3), channel_id=1, source_target_pairs={{0,1},{1,0},{2,3},{3,2},{4,5},{5,4},{6,7},{7,6},{8,9},{9,8},{10,11... | collective-permute-start | bytes 3538952 | tf_op jit(solution)/shard_map/ppermute | solution.py:146
  2.6 0.7 pad.4
  3.2 0.7 fusion
  4.0 10.9 %collective-permute-start.1 = (bf16[112,128]{1,0:T(8,128)(2,1)S(1)}, bf16[112,128]{1,0:T(8,128)(2,1)S(1)}, u32[]{:S(2)}, u32[]{:S(2)}) collective-permute-start(bf16[112,128]{1,0:T(8,128)(2,1)S(1)} %get-tuple-element.30), channel_id=1, source_target_pairs={{0,16},{16,32},{32,0},{1,17},{17,33},{33,1},{2,18},{18,34},{34,2},... | collective-permute-start | bytes 86024 | tf_op jit(solution)/shard_map/ppermute | solution.py:150
  14.9 5.6 %collective-permute-start.2 = (bf16[112,128]{1,0:T(8,128)(2,1)S(1)}, bf16[112,128]{1,0:T(8,128)(2,1)S(1)}, u32[]{:S(2)}, u32[]{:S(2)}) collective-permute-start(bf16[112,128]{1,0:T(8,128)(2,1)S(1)} %get-tuple-element.30), channel_id=1, source_target_pairs={{0,32},{16,0},{32,16},{1,33},{17,1},{33,17},{2,34},{18,2},{34,18},... | collective-permute-start | bytes 86024 | tf_op jit(solution)/shard_map/ppermute | solution.py:150
  20.5 0.0 copy-start
  20.5 1.3 %copy-done = bf16[128,4608]{1,0:T(8,128)(2,1)S(1)} copy-done((bf16[128,4608]{1,0:T(8,128)(2,1)S(1)}, bf16[128,4608]{1,0:T(8,128)(2,1)}, u32[]{:S(2)}) %copy-start) | copy-done | bytes 1179672
  21.7 0.0 copy-start.2
  21.7 0.8 copy-done.2
  22.5 1.1 %shard_map.67 = (f32[16,144,128]{2,1,0:T(8,128)S(1)}, f32[128,128]{1,0:T(8,128)S(1)}) custom-call(bf16[128,4608]{1,0:T(8,128)(2,1)S(1)} %copy-done, bf16[128,128]{1,0:T(8,128)(2,1)S(1)} %copy-done.2), custom_call_target="tpu_custom_call" | custom-call | flops 301989888 | bytes 2359296 | tf_op jit(solution)/shard_map/pallas_call | solution.py:159
  23.6 0.0 collective-permute-done.1
  23.6 1.8 %collective-permute-done.2 = bf16[112,128]{1,0:T(8,128)(2,1)S(1)} collective-permute-done((bf16[112,128]{1,0:T(8,128)(2,1)S(1)}, bf16[112,128]{1,0:T(8,128)(2,1)S(1)}, u32[]{:S(2)}, u32[]{:S(2)}) %collective-permute-start.2) | collective-permute-done | bytes 28704 | tf_op jit(solution)/shard_map/ppermute | solution.py:150
  25.4 2.8 %collective-permute-start.3 = (bf16[3,112,128]{2,1,0:T(8,128)(2,1)S(1)}, bf16[3,112,128]{2,1,0:T(8,128)(2,1)S(1)}, u32[]{:S(2)}, u32[]{:S(2)}) collective-permute-start(bf16[3,112,128]{2,1,0:T(8,128)(2,1)S(1)} %pad_maximum_fusion.2), channel_id=1, source_target_pairs={{0,2},{2,0},{4,6},{6,4},{8,10},{10,8},{12,14},{14,12},{1,3},{3,1},... | collective-permute-start | bytes 258056 | tf_op jit(solution)/shard_map/ppermute | solution.py:168
  28.3 1.9 %collective-permute-start.4 = (bf16[128,128]{1,0:T(8,128)(2,1)S(1)}, bf16[128,128]{1,0:T(8,128)(2,1)S(1)}, u32[]{:S(2)}, u32[]{:S(2)}) collective-permute-start(bf16[128,128]{1,0:T(8,128)(2,1)S(1)} %copy-done.2), channel_id=1, source_target_pairs={{0,1},{1,0},{2,3},{3,2},{4,5},{5,4},{6,7},{7,6},{8,9},{9,8},{10,11... | collective-permute-start | bytes 98312 | tf_op jit(solution)/shard_map/ppermute | solution.py:146
  30.2 0.0 collective-permute-done.x_ref
  30.2 1.2 %collective-permute-done.4.cot_ref = bf16[128,128]{1,0:T(8,128)(2,1)S(1)} collective-permute-done((bf16[128,128]{1,0:T(8,128)(2,1)S(1)}, bf16[128,128]{1,0:T(8,128)(2,1)S(1)}, u32[]{:S(2)}, u32[]{:S(2)}) %collective-permute-start.4) | collective-permute-done | bytes 32800 | tf_op jit(solution)/shard_map/ppermute | solution.py:146
  31.4 1.1 %shard_map.68 = f32[16,152,128]{2,1,0:T(8,128)S(1)} custom-call(bf16[128,4608]{1,0:T(8,128)(2,1)S(1)} %collective-permute-done.x_ref, bf16[128,128]{1,0:T(8,128)(2,1)S(1)} %collective-permute-done.4.cot_ref, bf16[128,128]{1,0:T(8,128)(2,1)S(1)} %copy-done.2, f32[16,144,128]{2,1,0:T(8,128)S(1)} %get-tuple-element.21.near_ref), custom_call_target="tpu_custom_call" | custom-call | flops 301989888 | bytes 3538944 | tf_op jit(solution)/shard_map/pallas_call | solution.py:170
  32.5 0.9 %convert_element_type.8 = f16[16,152,128]{2,1,0:T(8,128)(2,1)} convert(f32[16,152,128]{2,1,0:T(8,128)S(1)} %shard_map.68) | non-fusion elementwise | flops 311296 | bytes 1867776 | tf_op jit(solution)/shard_map/convert_element_type | solution.py:177
  33.4 0.0 collective-permute-done.3
  33.4 8.5 %all-to-all-start = ((f16[16,152,128]{2,1,0:T(8,128)(2,1)}), f16[16,152,128]{2,1,0:T(8,128)(2,1)S(1)}, u32[]{:S(2)}, u32[]{:S(2)}) async-start(f16[16,152,128]{2,1,0:T(8,128)(2,1)} %convert_element_type.8), calls=%async_computation | async-start | bytes 1245184 | tf_op jit(solution)/shard_map/all_to_all | solution.py:179
  41.9 7.7 %collective-permute-start.6 = (bf16[2,3,112,128]{3,2,1,0:T(8,128)(2,1)S(1)}, bf16[2,3,112,128]{3,2,1,0:T(8,128)(2,1)S(1)}, u32[]{:S(2)}, u32[]{:S(2)}) collective-permute-start(bf16[2,3,112,128]{3,2,1,0:T(8,128)(2,1)S(1)} %get-tuple-element.28), channel_id=1, source_target_pairs={{0,8},{2,10},{4,12},{6,14},{8,0},{10,2},{12,4},{14,6},{1,9},{3,11}... | collective-permute-start | bytes 516104 | tf_op jit(solution)/shard_map/ppermute | solution.py:150
  49.7 2.7 %collective-permute-start.5 = (bf16[2,3,112,128]{3,2,1,0:T(8,128)(2,1)S(1)}, bf16[2,3,112,128]{3,2,1,0:T(8,128)(2,1)S(1)}, u32[]{:S(2)}, u32[]{:S(2)}) collective-permute-start(bf16[2,3,112,128]{3,2,1,0:T(8,128)(2,1)S(1)} %get-tuple-element.28), channel_id=1, source_target_pairs={{0,4},{2,6},{4,8},{6,10},{8,12},{10,14},{12,0},{14,2},{1,5},{3,7},... | collective-permute-start | bytes 516104 | tf_op jit(solution)/shard_map/ppermute | solution.py:150
  52.4 5.2 %collective-permute-start.7 = (bf16[2,3,112,128]{3,2,1,0:T(8,128)(2,1)S(1)}, bf16[2,3,112,128]{3,2,1,0:T(8,128)(2,1)S(1)}, u32[]{:S(2)}, u32[]{:S(2)}) collective-permute-start(bf16[2,3,112,128]{3,2,1,0:T(8,128)(2,1)S(1)} %get-tuple-element.28), channel_id=1, source_target_pairs={{0,12},{2,14},{4,0},{6,2},{8,4},{10,6},{12,8},{14,10},{1,13},{3,15... | collective-permute-start | bytes 516104 | tf_op jit(solution)/shard_map/ppermute | solution.py:150
  57.6 3.2 %all-to-all-done = f16[16,152,128]{2,1,0:T(8,128)(2,1)S(1)} async-done(((f16[16,152,128]{2,1,0:T(8,128)(2,1)}), f16[16,152,128]{2,1,0:T(8,128)(2,1)S(1)}, u32[]{:S(2)}, u32[]{:S(2)}) %all-to-all-start) | async-done | bytes 622624 | tf_op jit(solution)/shard_map/all_to_all | solution.py:179
  60.9 0.1 convert_element_type.9.parts_ref
  60.9 0.8 shard_map.69
  61.7 11.2 %all-to-all-start.1 = ((f32[24,8,128]{2,1,0:T(8,128)}), f32[24,8,128]{2,1,0:T(8,128)S(1)}, u32[]{:S(2)}, u32[]{:S(2)}) async-start(f32[24,8,128]{2,1,0:T(8,128)} %shard_map.69), calls=%async_computation.1 | async-start | bytes 196608 | tf_op jit(solution)/shard_map/all_to_all | solution.py:183
  72.9 0.0 collective-permute-done.6
  72.9 0.0 collective-permute-done.5
  72.9 0.0 collective-permute-done.7
  72.9 0.1 pad_maximum_fusion.own_ref
  73.0 0.0 copy-start.1
  73.0 0.0 copy-start.3
  73.0 2.1 %collective-permute-start.8 = (bf16[4,2,3,112,128]{4,3,2,1,0:T(8,128)(2,1)S(1)}, bf16[4,2,3,112,128]{4,3,2,1,0:T(8,128)(2,1)S(1)}, u32[]{:S(2)}, u32[]{:S(2)}) collective-permute-start(bf16[4,2,3,112,128]{4,3,2,1,0:T(8,128)(2,1)S(1)} %pad_maximum_fusion.own_ref), channel_id=1, source_target_pairs={{0,1},{1,0},{2,3},{3,2},{4,5},{5,4},{6,7},{7,6},{8,9},{9,8},{10,11... | collective-permute-start | bytes 2064392 | tf_op jit(solution)/shard_map/ppermute | solution.py:146
  75.1 9.3 %all-to-all-done.1.parts_ref = f32[24,8,128]{2,1,0:T(8,128)S(1)} async-done(((f32[24,8,128]{2,1,0:T(8,128)}), f32[24,8,128]{2,1,0:T(8,128)S(1)}, u32[]{:S(2)}, u32[]{:S(2)}) %all-to-all-start.1) | async-done | bytes 98336 | tf_op jit(solution)/shard_map/all_to_all | solution.py:183
  84.4 0.0 collective-permute-done.8.other_ref
  84.4 0.0 copy-done.1
  84.4 0.0 copy-done.3
  84.4 2.6 %shard_map.71 = (bf16[128,4608]{1,0:T(8,128)(2,1)}, f32[6,128]{1,0:T(8,128)}, f32[6]{0:T(128)}) custom-call(bf16[128,4608]{1,0:T(8,128)(2,1)S(1)} %copy-done.1, bf16[128,128]{1,0:T(8,128)(2,1)S(1)} %copy-done.3, f32[128,128]{1,0:T(8,128)S(1)} %get-tuple-element.15.inv_ref, bf16[4,2,3,112,128]{4,3,2,1,0:T(8,128)(2,1)S(1)} %pad_maximum_fusion.own_ref, ...), custom_call_target="tpu_custom_call" | custom-call | flops 150994944 | bytes 2359296 | tf_op jit(solution)/shard_map/pallas_call | solution.py:189
  (4 shorter events, 0.1 us)
Async XLA Ops:
  0.6 29.6 %collective-permute-start = (bf16[128,4608]{1,0:T(8,128)(2,1)}, bf16[128,4608]{1,0:T(8,128)(2,1)S(1)}, u32[]{:S(2)}, u32[]{:S(2)}) collective-permute-start(bf16[128,4608]{1,0:T(8,128)(2,1)} %x_ref.3), channel_id=1, source_target_pairs={{0,1},{1,0},{2,3},{3,2},{4,5},{5,4},{6,7},{7,6},{8,9},{9,8},{10,11... | collective-permute-start | bytes 3538952 | tf_op jit(solution)/shard_map/ppermute | solution.py:146
  4.0 19.6 %collective-permute-start.1 = (bf16[112,128]{1,0:T(8,128)(2,1)S(1)}, bf16[112,128]{1,0:T(8,128)(2,1)S(1)}, u32[]{:S(2)}, u32[]{:S(2)}) collective-permute-start(bf16[112,128]{1,0:T(8,128)(2,1)S(1)} %get-tuple-element.30), channel_id=1, source_target_pairs={{0,16},{16,32},{32,0},{1,17},{17,33},{33,1},{2,18},{18,34},{34,2},... | collective-permute-start | bytes 86024 | tf_op jit(solution)/shard_map/ppermute | solution.py:150
  14.9 10.5 %collective-permute-start.2 = (bf16[112,128]{1,0:T(8,128)(2,1)S(1)}, bf16[112,128]{1,0:T(8,128)(2,1)S(1)}, u32[]{:S(2)}, u32[]{:S(2)}) collective-permute-start(bf16[112,128]{1,0:T(8,128)(2,1)S(1)} %get-tuple-element.30), channel_id=1, source_target_pairs={{0,32},{16,0},{32,16},{1,33},{17,1},{33,17},{2,34},{18,2},{34,18},... | collective-permute-start | bytes 86024 | tf_op jit(solution)/shard_map/ppermute | solution.py:150
  20.5 1.3 %copy-start = (bf16[128,4608]{1,0:T(8,128)(2,1)S(1)}, bf16[128,4608]{1,0:T(8,128)(2,1)}, u32[]{:S(2)}) copy-start(bf16[128,4608]{1,0:T(8,128)(2,1)} %x_ref.3) | copy-start | bytes 3538948
  21.7 0.8 copy-start.2
  25.4 7.9 %collective-permute-start.3 = (bf16[3,112,128]{2,1,0:T(8,128)(2,1)S(1)}, bf16[3,112,128]{2,1,0:T(8,128)(2,1)S(1)}, u32[]{:S(2)}, u32[]{:S(2)}) collective-permute-start(bf16[3,112,128]{2,1,0:T(8,128)(2,1)S(1)} %pad_maximum_fusion.2), channel_id=1, source_target_pairs={{0,2},{2,0},{4,6},{6,4},{8,10},{10,8},{12,14},{14,12},{1,3},{3,1},... | collective-permute-start | bytes 258056 | tf_op jit(solution)/shard_map/ppermute | solution.py:168
  28.3 3.1 %collective-permute-start.4 = (bf16[128,128]{1,0:T(8,128)(2,1)S(1)}, bf16[128,128]{1,0:T(8,128)(2,1)S(1)}, u32[]{:S(2)}, u32[]{:S(2)}) collective-permute-start(bf16[128,128]{1,0:T(8,128)(2,1)S(1)} %copy-done.2), channel_id=1, source_target_pairs={{0,1},{1,0},{2,3},{3,2},{4,5},{5,4},{6,7},{7,6},{8,9},{9,8},{10,11... | collective-permute-start | bytes 98312 | tf_op jit(solution)/shard_map/ppermute | solution.py:146
  33.4 27.5 %all-to-all-start = ((f16[16,152,128]{2,1,0:T(8,128)(2,1)}), f16[16,152,128]{2,1,0:T(8,128)(2,1)S(1)}, u32[]{:S(2)}, u32[]{:S(2)}) async-start(f16[16,152,128]{2,1,0:T(8,128)(2,1)} %convert_element_type.8), calls=%async_computation | async-start | bytes 1245184 | tf_op jit(solution)/shard_map/all_to_all | solution.py:179
  41.9 30.9 %collective-permute-start.6 = (bf16[2,3,112,128]{3,2,1,0:T(8,128)(2,1)S(1)}, bf16[2,3,112,128]{3,2,1,0:T(8,128)(2,1)S(1)}, u32[]{:S(2)}, u32[]{:S(2)}) collective-permute-start(bf16[2,3,112,128]{3,2,1,0:T(8,128)(2,1)S(1)} %get-tuple-element.28), channel_id=1, source_target_pairs={{0,8},{2,10},{4,12},{6,14},{8,0},{10,2},{12,4},{14,6},{1,9},{3,11}... | collective-permute-start | bytes 516104 | tf_op jit(solution)/shard_map/ppermute | solution.py:150
  49.7 23.2 %collective-permute-start.5 = (bf16[2,3,112,128]{3,2,1,0:T(8,128)(2,1)S(1)}, bf16[2,3,112,128]{3,2,1,0:T(8,128)(2,1)S(1)}, u32[]{:S(2)}, u32[]{:S(2)}) collective-permute-start(bf16[2,3,112,128]{3,2,1,0:T(8,128)(2,1)S(1)} %get-tuple-element.28), channel_id=1, source_target_pairs={{0,4},{2,6},{4,8},{6,10},{8,12},{10,14},{12,0},{14,2},{1,5},{3,7},... | collective-permute-start | bytes 516104 | tf_op jit(solution)/shard_map/ppermute | solution.py:150
  52.4 20.5 %collective-permute-start.7 = (bf16[2,3,112,128]{3,2,1,0:T(8,128)(2,1)S(1)}, bf16[2,3,112,128]{3,2,1,0:T(8,128)(2,1)S(1)}, u32[]{:S(2)}, u32[]{:S(2)}) collective-permute-start(bf16[2,3,112,128]{3,2,1,0:T(8,128)(2,1)S(1)} %get-tuple-element.28), channel_id=1, source_target_pairs={{0,12},{2,14},{4,0},{6,2},{8,4},{10,6},{12,8},{14,10},{1,13},{3,15... | collective-permute-start | bytes 516104 | tf_op jit(solution)/shard_map/ppermute | solution.py:150
  61.7 22.7 %all-to-all-start.1 = ((f32[24,8,128]{2,1,0:T(8,128)}), f32[24,8,128]{2,1,0:T(8,128)S(1)}, u32[]{:S(2)}, u32[]{:S(2)}) async-start(f32[24,8,128]{2,1,0:T(8,128)} %shard_map.69), calls=%async_computation.1 | async-start | bytes 196608 | tf_op jit(solution)/shard_map/all_to_all | solution.py:183
  73.0 11.4 %copy-start.1 = (bf16[128,4608]{1,0:T(8,128)(2,1)S(1)}, bf16[128,4608]{1,0:T(8,128)(2,1)}, u32[]{:S(2)}) copy-start(bf16[128,4608]{1,0:T(8,128)(2,1)} %x_ref.3) | copy-start | bytes 3538948
  73.0 11.4 %copy-start.3 = (bf16[128,128]{1,0:T(8,128)(2,1)S(1)}, bf16[128,128]{1,0:T(8,128)(2,1)}, u32[]{:S(2)}) copy-start(bf16[128,128]{1,0:T(8,128)(2,1)} %cot_ref.3) | copy-start | bytes 98308
  73.0 11.4 %collective-permute-start.8 = (bf16[4,2,3,112,128]{4,3,2,1,0:T(8,128)(2,1)S(1)}, bf16[4,2,3,112,128]{4,3,2,1,0:T(8,128)(2,1)S(1)}, u32[]{:S(2)}, u32[]{:S(2)}) collective-permute-start(bf16[4,2,3,112,128]{4,3,2,1,0:T(8,128)(2,1)S(1)} %pad_maximum_fusion.own_ref), channel_id=1, source_target_pairs={{0,1},{1,0},{2,3},{3,2},{4,5},{5,4},{6,7},{7,6},{8,9},{9,8},{10,11... | collective-permute-start | bytes 2064392 | tf_op jit(solution)/shard_map/ppermute | solution.py:146

commit v3 on v2

--- a/solution.py
+++ b/solution.py
@@ -7,14 +7,14 @@
 
 EPS = 1e-05
 X, ZL, ZH, Y, C = 4, 4, 3, 8, 2
-INTER, PEERS = X * ZL, ZH * Y
-DEVICES = INTER * PEERS * C
+PLANE, LINE = X * Y, ZL * ZH
+DEVICES = PLANE * LINE * C
 TOK, D, H = 128, 4608, 128
 ROWS = D // DEVICES
-SHARD = D // (PEERS * C)
+SHARD = D // (ZH * Y * C)
 SLAB = SHARD + 16
 HALF = D // C
-PART = HALF // INTER
+PART = HALF // PLANE
 CHUNK = 512
 BF16, F16, F32 = jnp.bfloat16, jnp.float16, jnp.float32
 VMEM = pl.BlockSpec(memory_space=pltpu.VMEM)
@@ -38,8 +38,15 @@
         all_ref[at : at + CHUNK, :] = pair[:, :H] + pair[:, H:]
 
 
-def rows_of(all_ref, group, row, core):
-    return all_ref[pl.ds(group * C * PART + row + core * ROWS, PEERS, stride=C * ROWS), :]
+def rows_of(all_ref, chip, row, core, first, count):
+    start = chip // Y * (D // X) + chip % Y * (C * ROWS) + row + first * SHARD
+    return all_ref[pl.ds(start + core * ROWS, count, stride=SHARD), :]
+
+
+def pieces():
+    for row in range(ROWS):
+        for first, count in ((0, 8), (8, 4)) if row % 2 == 0 else ((0, 4), (4, 8)):
+            yield row, first, count, row * LINE + first
 
 
 def near_terms(x_ref, cot_ref, half_ref, inv_ref, all_ref):
@@ -47,9 +54,9 @@
     inv_ref[...] = jnp.broadcast_to(inv, (TOK, 128))
     products(x_ref, cot_ref[...].astype(F32) * inv, all_ref)
     mine = lax.axis_index("core")
-    for group in range(INTER):
-        for row in range(ROWS):
-            half_ref[group, row * PEERS : (row + 1) * PEERS, :] = rows_of(all_ref, group, row, mine)
+    for chip in range(PLANE):
+        for row, first, count, at in pieces():
+            half_ref[chip, at : at + count, :] = rows_of(all_ref, chip, row, mine, first, count)
 
 
 def far_terms(x_ref, cot_ref, near_cot_ref, near_ref, half_ref, all_ref):
@@ -59,35 +66,32 @@
     scale = jnp.exp2(-power)
     products(x_ref, cot * (inverse(x_ref) * scale), all_ref)
     mine = lax.axis_index("core")
-    for group in range(INTER):
-        for row in range(ROWS):
-            to = slice(row * PEERS, (row + 1) * PEERS)
-            half_ref[group, to, :] = rows_of(all_ref, group, row, mine) + near_ref[group, to, :] * scale
-        half_ref[group, PART:, :] = jnp.broadcast_to(power, (8, H))
-
-
-def group_sum(parts_ref, out_ref, sum_ref):
+    for chip in range(PLANE):
+        for row, first, count, at in pieces():
+            to = slice(at, at + count)
+            half_ref[chip, to, :] = rows_of(all_ref, chip, row, mine, first, count) + near_ref[chip, to, :] * scale
+        half_ref[chip, PART:, :] = jnp.broadcast_to(power, (8, H))
+
+
+def plane_sum(parts_ref, out_ref, sum_ref):
     total = jnp.zeros((PART, H), F32)
-    for group in range(INTER):
-        total += parts_ref[group, :PART] * jnp.exp2(parts_ref[group, PART : PART + 1, :])
+    for chip in range(PLANE):
+        total += parts_ref[chip, :PART] * jnp.exp2(parts_ref[chip, PART : PART + 1, :])
     sum_ref[:PART, :] = total
-    sum_ref[PART:, :] = jnp.zeros((8 * PEERS - PART, H), F32)
-    for peer in range(PEERS):
-        out_ref[peer] = sum_ref[pl.ds(peer, 8, stride=PEERS), :]
+    sum_ref[PART:, :] = jnp.zeros((8 * LINE - PART, H), F32)
+    for place in range(LINE):
+        out_ref[place] = sum_ref[pl.ds(place, 8, stride=LINE), :]
 
 
 def outputs(x_ref, cot_ref, inv_ref, own_ref, other_ref, total_ref, grad_ref, weight_ref, gain_ref, w_ref, g_ref, sg_ref, win_ref):
     mine, my_y, my_zh = lax.axis_index("core"), lax.axis_index("y"), lax.axis_index("zh")
-    for hop in range(Y // 2):
-        base_y = lax.rem(my_y + Y - 2 * hop, Y)
-        for side in range(2):
-            from_y = base_y if side == 0 else base_y + 1 - 2 * lax.rem(base_y, 2)
-            for turn in range(ZH):
-                peer = lax.rem(my_zh + ZH - turn, ZH) * Y + from_y
-                for ref, core in ((own_ref, mine), (other_ref, 1 - mine)):
-                    shard = 2 * peer + core
-                    w_ref[pl.ds(pl.multiple_of(shard * SHARD, SHARD), SHARD), :] = ref[hop, side, turn, :SHARD, :]
-                    g_ref[lax.rem(shard, 4), pl.ds(shard // 4, 1), :] = ref[hop, side, turn, SHARD:, :].astype(F32)[:1]
+    for turn in range(ZH):
+        from_zh = lax.rem(my_zh + ZH - turn, ZH)
+        for y in range(Y):
+            for ref, core in ((own_ref, mine), (other_ref, 1 - mine)):
+                shard = 2 * (from_zh * Y + y) + core
+                w_ref[pl.ds(pl.multiple_of(shard * SHARD, SHARD), SHARD), :] = ref[turn, y, :SHARD, :]
+                g_ref[lax.rem(shard, 4), pl.ds(shard // 4, 1), :] = ref[turn, y, SHARD:, :].astype(F32)[:1]
     w_ref[D:, :] = jnp.zeros((32, H), BF16)
     lane = lax.broadcasted_iota(jnp.int32, (16, 128), 1)
     g0, g1, g2, g3 = g_ref[0], g_ref[1], g_ref[2], g_ref[3]
@@ -96,7 +100,7 @@
         jnp.where(lane < 64, pltpu.roll(g1, 96, 1), pltpu.roll(g2, 64, 1)),
         jnp.where(lane < 32, pltpu.roll(g2, 64, 1), pltpu.roll(g3, 32, 1)),
     )
-    first = ((lax.axis_index("x") * ZL + lax.axis_index("zl")) * PEERS + my_zh * Y + my_y) * C
+    first = ((lax.axis_index("x") * ZL + lax.axis_index("zl")) * (ZH * Y) + my_zh * Y + my_y) * C
     first = (first + mine) * ROWS
     base = pl.multiple_of(first // 16 * 16, 16)
     win_ref[:32, :] = w_ref[pl.ds(base, 32), :].astype(F32)
@@ -127,8 +131,8 @@
 
 def last_sum(parts_ref, total_ref):
     total = parts_ref[0]
-    for peer in range(1, PEERS):
-        total += parts_ref[peer]
+    for place in range(1, LINE):
+        total += parts_ref[place]
     total_ref[...] = total * (1.0 / DEVICES)
 
 
@@ -146,46 +150,42 @@
     return lax.ppermute(a, "core", [(0, 1), (1, 0)])
 
 
+def exchange(a, axis):
+    return lax.all_to_all(a, axis, split_axis=0, concat_axis=0, tiled=True)
+
+
 def shift(a, axis, n, by):
     return lax.ppermute(a, axis, [(i, (i + by) % n) for i in range(n)])
 
 
 def on_device(layer_input, norm_gain, kv_weight, kv_cotangent):
-    barrier = lax.optimization_barrier
     far, far_cot = swap_cores(layer_input), swap_cores(kv_cotangent)
     gains = jnp.broadcast_to(jnp.pad(norm_gain, (0, 128 - SHARD))[None], (16, 128))
     slab = jnp.concatenate([kv_weight, gains], axis=0)
-    turns = [shift(slab, "zh", ZH, turn) for turn in range(1, ZH)]
+    column = exchange(jnp.broadcast_to(slab[None], (Y, SLAB, H)), "y")
+    turns = [shift(column, "zh", ZH, turn) for turn in range(1, ZH)]
     near, inv = call(
         near_terms,
-        [((INTER, PART, H), F32), ((TOK, 128), F32)],
+        [((PLANE, PART, H), F32), ((TOK, 128), F32)],
         [pltpu.VMEM((D, H), F32)],
         flops=4 * TOK * D * H,
         moved=2 * TOK * D + 2 * D * H,
     )(layer_input, kv_cotangent)
-    turns, near = barrier((turns, near))
-    column = jnp.stack([slab] + turns)
-    beside = lax.ppermute(column, "y", [(i, i ^ 1) for i in range(Y)])
-    far, column = barrier((far, column))
     (half,) = call(
         far_terms,
-        [((INTER, PART + 8, H), F32)],
+        [((PLANE, PART + 8, H), F32)],
         [pltpu.VMEM((D, H), F32)],
         flops=4 * TOK * D * H,
         moved=2 * TOK * D + 4 * D * H,
     )(far, far_cot, kv_cotangent, near)
-    short = half.astype(F16)
-    beside, short = barrier((beside, short))
-    parts = lax.all_to_all(short, ("x", "zl"), split_axis=0, concat_axis=0, tiled=True).astype(F32)
-    two = jnp.stack([column, beside])
-    hops = [shift(two, "y", Y, 2 * hop) for hop in range(1, Y // 2)]
-    (sums,) = call(group_sum, [((PEERS, 8, H), F32)], [pltpu.VMEM((8 * PEERS, H), F32)], flops=INTER * PART * H, moved=4 * HALF * H)(parts)
-    last = lax.all_to_all(sums, ("zh", "y"), split_axis=0, concat_axis=0, tiled=True)
-    hops, _ = barrier((hops, sums))
-    own = jnp.stack([two] + hops)
+    parts = exchange(half.astype(F16), ("x", "y")).astype(F32)
+    (sums,) = call(plane_sum, [((LINE, 8, H), F32)], [pltpu.VMEM((8 * LINE, H), F32)], flops=PLANE * PART * H, moved=4 * HALF * H)(parts)
+    last = exchange(sums, ("zl", "zh"))
+    turns, _ = lax.optimization_barrier((turns, sums))
+    own = jnp.stack([column] + turns)
     other = swap_cores(own)
 
-    (total,) = call(last_sum, [((8, H), F32)], flops=int(2e10), moved=PEERS * 4096)(last)
+    (total,) = call(last_sum, [((8, H), F32)], flops=int(2e10), moved=LINE * 4096)(last)
     return call(
         outputs,
         [((TOK, D), BF16), ((ROWS, H), F32), ((ROWS,), F32)],

time: 87.7 us -> 81.8 us (0.933)
  starting transfers between devices: 60.5 us -> 50.2 us
  waiting for transfers between devices: 15.5 us -> 17.9 us
  Pallas kernels: 5.57 us -> 6.94 us
    ppermute x5 -> x2, starting transfers between devices: 32.1 us -> 13.5 us  [shift(): return lax.ppermute(a, axis, [(i, (i + by) % n) for i in range(n)])]
    all_to_all x2 -> x3, starting transfers between devices: 19.7 us -> 30.6 us  [exchange(): return lax.all_to_all(a, axis, split_axis=0, concat_axis=0, tiled=True)]
    all_to_all x2 -> x3, waiting for transfers between devices: 12.5 us -> 17.9 us  [exchange(): return lax.all_to_all(a, axis, split_axis=0, concat_axis=0, tiled=True)]
    ppermute x1 -> x0, starting transfers between devices: 2.82 us -> none  [on_device(): beside = lax.ppermute(column, 'y', [(i, i ^ 1) for i in range(Y)])]
    ppermute x5 -> x2, waiting for transfers between devices: 1.85 us -> 0.01 us  [shift(): return lax.ppermute(a, axis, [(i, (i + by) % n) for i in range(n)])]
    pallas_call x4, Pallas kernels: 2.96 us -> 4.35 us  [the longest x1 1.88 us: on_device(): call(far_terms, [((PLANE, PART + 8, H), F32)], [pltpu.VMEM((D, H), F32)],...]
    ppermute x3, waiting for transfers between devices: 1.17 us -> 0.01 us  [swap_cores(): return lax.ppermute(a, 'core', [(0, 1), (1, 0)])]
  transfers between devices with their start and end apart: 11 -> 8, of which waited for: 4 -> 3; matrix products, arithmetic and copies ran while one was open for 3% -> 4% of each run, Pallas kernels for 3% -> 5%
where the time goes in v3:
time: 81.8 us; the launch traced here: 81.1 us
  starting transfers between devices  50.2 us (61%)
  waiting for transfers between devices  17.9 us (22%)
  Pallas kernels  6.94 us (8%)
  local copies, waits for them, and re-layouts  3.42 us (4%)
  other arithmetic  1.83 us (2%)
    all_to_all x3, starting transfers between devices, exchange(): return lax.all_to_all(a, axis, split_axis=0, concat_axis=0, tiled=True)  30.6 us
    all_to_all x3, waiting for transfers between devices, exchange(): return lax.all_to_all(a, axis, split_axis=0, concat_axis=0, tiled=True)  17.9 us
    ppermute x2, starting transfers between devices, shift(): return lax.ppermute(a, axis, [(i, (i + by) % n) for i in range(n)])  13.5 us
    ppermute x3, starting transfers between devices, swap_cores(): return lax.ppermute(a, 'core', [(0, 1), (1, 0)])  6.09 us
    pallas_call x1, Pallas kernels, on_device(): call(outputs, [((TOK, D), BF16), ((ROWS, H), F32), ((ROWS,), F32)], [pltp...  2.59 us
    unnamed x8, local copies, waits for them, and re-layouts  2.04 us
    pallas_call x1, Pallas kernels, on_device(): call(far_terms, [((PLANE, PART + 8, H), F32)], [pltpu.VMEM((D, H), F32)],...  1.88 us
    pallas_call x1, Pallas kernels, on_device(): call(near_terms, [((PLANE, PART, H), F32), ((TOK, 128), F32)], [pltpu.VME...  1.73 us
  transfers between devices with their start and end apart: 8, of which 3 were waited for; matrix products, arithmetic and copies ran while one was open for 4% of the time, Pallas kernels for 5%

profile of v3, /device:TPU:8, one launch (start us, length us, event | category | flops | bytes accessed | tf_op | source)
XLA Modules:
  0.0 81.1 jit_solution(14995163498096039793)
XLA Ops:
  0.6 1.9 %collective-permute-start.2 = (bf16[128,4608]{1,0:T(8,128)(2,1)}, bf16[128,4608]{1,0:T(8,128)(2,1)S(1)}, u32[]{:S(2)}, u32[]{:S(2)}) collective-permute-start(bf16[128,4608]{1,0:T(8,128)(2,1)} %x_ref.3), channel_id=1, source_target_pairs={{0,1},{1,0},{2,3},{3,2},{4,5},{5,4},{6,7},{7,6},{8,9},{9,8},{10,11... | collective-permute-start | bytes 3538952 | tf_op jit(solution)/shard_map/ppermute | solution.py:150
  2.6 0.7 pad.4
  3.2 0.7 pad_maximum_fusion.1
  4.0 0.7 broadcast_in_dim.5
  4.7 12.8 %all-to-all-start = ((bf16[8,112,128]{2,1,0:T(8,128)(2,1)}), bf16[8,112,128]{2,1,0:T(8,128)(2,1)S(1)}, u32[]{:S(2)}, u32[]{:S(2)}) async-start(bf16[8,112,128]{2,1,0:T(8,128)(2,1)} %broadcast_in_dim.5), calls=%async_computation | async-start | bytes 458752 | tf_op jit(solution)/shard_map/all_to_all | solution.py:154
  17.4 2.1 %collective-permute-start.3 = (bf16[128,128]{1,0:T(8,128)(2,1)}, bf16[128,128]{1,0:T(8,128)(2,1)S(1)}, u32[]{:S(2)}, u32[]{:S(2)}) collective-permute-start(bf16[128,128]{1,0:T(8,128)(2,1)} %cot_ref.3), channel_id=1, source_target_pairs={{0,1},{1,0},{2,3},{3,2},{4,5},{5,4},{6,7},{7,6},{8,9},{9,8},{10,11... | collective-permute-start | bytes 98312 | tf_op jit(solution)/shard_map/ppermute | solution.py:150
  19.6 0.0 copy-start
  19.6 1.3 %copy-done = bf16[128,4608]{1,0:T(8,128)(2,1)S(1)} copy-done((bf16[128,4608]{1,0:T(8,128)(2,1)S(1)}, bf16[128,4608]{1,0:T(8,128)(2,1)}, u32[]{:S(2)}) %copy-start) | copy-done | bytes 1179672
  20.8 0.0 copy-start.2
  20.8 0.8 copy-done.2
  21.6 1.7 %shard_map.67 = (f32[32,72,128]{2,1,0:T(8,128)S(1)}, f32[128,128]{1,0:T(8,128)S(1)}) custom-call(bf16[128,4608]{1,0:T(8,128)(2,1)S(1)} %copy-done, bf16[128,128]{1,0:T(8,128)(2,1)S(1)} %copy-done.2), custom_call_target="tpu_custom_call" | custom-call | flops 301989888 | bytes 2359296 | tf_op jit(solution)/shard_map/pallas_call | solution.py:167
  23.3 0.0 collective-permute-done.3.cot_ref
  23.4 0.0 collective-permute-done.2.x_ref
  23.4 1.9 %shard_map.68 = f32[32,80,128]{2,1,0:T(8,128)S(1)} custom-call(bf16[128,4608]{1,0:T(8,128)(2,1)S(1)} %collective-permute-done.2.x_ref, bf16[128,128]{1,0:T(8,128)(2,1)S(1)} %collective-permute-done.3.cot_ref, bf16[128,128]{1,0:T(8,128)(2,1)S(1)} %copy-done.2, f32[32,72,128]{2,1,0:T(8,128)S(1)} %get-tuple-element.8.near_ref), custom_call_target="tpu_custom_call" | custom-call | flops 301989888 | bytes 3538944 | tf_op jit(solution)/shard_map/pallas_call | solution.py:174
  25.3 0.9 %convert_element_type.8 = f16[32,80,128]{2,1,0:T(8,128)(2,1)} convert(f32[32,80,128]{2,1,0:T(8,128)S(1)} %shard_map.68) | non-fusion elementwise | flops 327680 | bytes 1966080 | tf_op jit(solution)/shard_map/convert_element_type | solution.py:181
  26.2 1.9 %all-to-all-done = bf16[8,112,128]{2,1,0:T(8,128)(2,1)S(1)} async-done(((bf16[8,112,128]{2,1,0:T(8,128)(2,1)}), bf16[8,112,128]{2,1,0:T(8,128)(2,1)S(1)}, u32[]{:S(2)}, u32[]{:S(2)}) %all-to-all-start) | async-done | bytes 229408 | tf_op jit(solution)/shard_map/all_to_all | solution.py:154
  28.1 5.4 %all-to-all-start.1 = ((f16[32,80,128]{2,1,0:T(8,128)(2,1)}), f16[32,80,128]{2,1,0:T(8,128)(2,1)S(1)}, u32[]{:S(2)}, u32[]{:S(2)}) async-start(f16[32,80,128]{2,1,0:T(8,128)(2,1)} %convert_element_type.8), calls=%async_computation.1 | async-start | bytes 1310720 | tf_op jit(solution)/shard_map/all_to_all | solution.py:154
  33.6 7.9 %collective-permute-start = (bf16[8,112,128]{2,1,0:T(8,128)(2,1)S(1)}, bf16[8,112,128]{2,1,0:T(8,128)(2,1)S(1)}, u32[]{:S(2)}, u32[]{:S(2)}) collective-permute-start(bf16[8,112,128]{2,1,0:T(8,128)(2,1)S(1)} %all-to-all-done), channel_id=1, source_target_pairs={{0,16},{16,32},{32,0},{1,17},{17,33},{33,1},{2,18},{18,34},{34,2},... | collective-permute-start | bytes 688136 | tf_op jit(solution)/shard_map/ppermute | solution.py:158
  41.5 5.6 %collective-permute-start.1 = (bf16[8,112,128]{2,1,0:T(8,128)(2,1)S(1)}, bf16[8,112,128]{2,1,0:T(8,128)(2,1)S(1)}, u32[]{:S(2)}, u32[]{:S(2)}) collective-permute-start(bf16[8,112,128]{2,1,0:T(8,128)(2,1)S(1)} %all-to-all-done), channel_id=1, source_target_pairs={{0,32},{16,0},{32,16},{1,33},{17,1},{33,17},{2,34},{18,2},{34,18},... | collective-permute-start | bytes 688136 | tf_op jit(solution)/shard_map/ppermute | solution.py:158
  47.1 7.3 %all-to-all-done.1 = f16[32,80,128]{2,1,0:T(8,128)(2,1)S(1)} async-done(((f16[32,80,128]{2,1,0:T(8,128)(2,1)}), f16[32,80,128]{2,1,0:T(8,128)(2,1)S(1)}, u32[]{:S(2)}, u32[]{:S(2)}) %all-to-all-start.1) | async-done | bytes 655392 | tf_op jit(solution)/shard_map/all_to_all | solution.py:154
  54.4 0.1 convert_element_type.9.parts_ref
  54.4 0.7 shard_map.69
  55.2 12.4 %all-to-all-start.2 = ((f32[12,8,128]{2,1,0:T(8,128)}), f32[12,8,128]{2,1,0:T(8,128)S(1)}, u32[]{:S(2)}, u32[]{:S(2)}) async-start(f32[12,8,128]{2,1,0:T(8,128)} %shard_map.69), calls=%async_computation.2 | async-start | bytes 98304 | tf_op jit(solution)/shard_map/all_to_all | solution.py:154
  67.6 0.0 collective-permute-done
  67.6 0.0 collective-permute-done.1
  67.6 0.1 pad_maximum_fusion.own_ref
  67.7 0.0 copy-start.1
  67.7 0.0 copy-start.3
  67.8 2.1 %collective-permute-start.4 = (bf16[3,8,112,128]{3,2,1,0:T(8,128)(2,1)S(1)}, bf16[3,8,112,128]{3,2,1,0:T(8,128)(2,1)S(1)}, u32[]{:S(2)}, u32[]{:S(2)}) collective-permute-start(bf16[3,8,112,128]{3,2,1,0:T(8,128)(2,1)S(1)} %pad_maximum_fusion.own_ref), channel_id=1, source_target_pairs={{0,1},{1,0},{2,3},{3,2},{4,5},{5,4},{6,7},{7,6},{8,9},{9,8},{10,11... | collective-permute-start | bytes 2064392 | tf_op jit(solution)/shard_map/ppermute | solution.py:150
  69.8 8.6 %all-to-all-done.2.parts_ref = f32[12,8,128]{2,1,0:T(8,128)S(1)} async-done(((f32[12,8,128]{2,1,0:T(8,128)}), f32[12,8,128]{2,1,0:T(8,128)S(1)}, u32[]{:S(2)}, u32[]{:S(2)}) %all-to-all-start.2) | async-done | bytes 49184 | tf_op jit(solution)/shard_map/all_to_all | solution.py:154
  78.5 0.0 collective-permute-done.4.other_ref
  78.5 0.0 copy-done.1
  78.5 0.0 copy-done.3
  78.5 2.6 %shard_map.71 = (bf16[128,4608]{1,0:T(8,128)(2,1)}, f32[6,128]{1,0:T(8,128)}, f32[6]{0:T(128)}) custom-call(bf16[128,4608]{1,0:T(8,128)(2,1)S(1)} %copy-done.1, bf16[128,128]{1,0:T(8,128)(2,1)S(1)} %copy-done.3, f32[128,128]{1,0:T(8,128)S(1)} %get-tuple-element.7.inv_ref, bf16[3,8,112,128]{3,2,1,0:T(8,128)(2,1)S(1)} %pad_maximum_fusion.own_ref, ...), custom_call_target="tpu_custom_call" | custom-call | flops 150994944 | bytes 2359296 | tf_op jit(solution)/shard_map/pallas_call | solution.py:189
  (2 shorter events, 0.0 us)
Async XLA Ops:
  0.6 22.7 %collective-permute-start.2 = (bf16[128,4608]{1,0:T(8,128)(2,1)}, bf16[128,4608]{1,0:T(8,128)(2,1)S(1)}, u32[]{:S(2)}, u32[]{:S(2)}) collective-permute-start(bf16[128,4608]{1,0:T(8,128)(2,1)} %x_ref.3), channel_id=1, source_target_pairs={{0,1},{1,0},{2,3},{3,2},{4,5},{5,4},{6,7},{7,6},{8,9},{9,8},{10,11... | collective-permute-start | bytes 3538952 | tf_op jit(solution)/shard_map/ppermute | solution.py:150
  4.7 23.5 %all-to-all-start = ((bf16[8,112,128]{2,1,0:T(8,128)(2,1)}), bf16[8,112,128]{2,1,0:T(8,128)(2,1)S(1)}, u32[]{:S(2)}, u32[]{:S(2)}) async-start(bf16[8,112,128]{2,1,0:T(8,128)(2,1)} %broadcast_in_dim.5), calls=%async_computation | async-start | bytes 458752 | tf_op jit(solution)/shard_map/all_to_all | solution.py:154
  17.4 5.9 %collective-permute-start.3 = (bf16[128,128]{1,0:T(8,128)(2,1)}, bf16[128,128]{1,0:T(8,128)(2,1)S(1)}, u32[]{:S(2)}, u32[]{:S(2)}) collective-permute-start(bf16[128,128]{1,0:T(8,128)(2,1)} %cot_ref.3), channel_id=1, source_target_pairs={{0,1},{1,0},{2,3},{3,2},{4,5},{5,4},{6,7},{7,6},{8,9},{9,8},{10,11... | collective-permute-start | bytes 98312 | tf_op jit(solution)/shard_map/ppermute | solution.py:150
  19.6 1.3 %copy-start = (bf16[128,4608]{1,0:T(8,128)(2,1)S(1)}, bf16[128,4608]{1,0:T(8,128)(2,1)}, u32[]{:S(2)}) copy-start(bf16[128,4608]{1,0:T(8,128)(2,1)} %x_ref.3) | copy-start | bytes 3538948
  20.8 0.8 copy-start.2
  28.1 26.2 %all-to-all-start.1 = ((f16[32,80,128]{2,1,0:T(8,128)(2,1)}), f16[32,80,128]{2,1,0:T(8,128)(2,1)S(1)}, u32[]{:S(2)}, u32[]{:S(2)}) async-start(f16[32,80,128]{2,1,0:T(8,128)(2,1)} %convert_element_type.8), calls=%async_computation.1 | async-start | bytes 1310720 | tf_op jit(solution)/shard_map/all_to_all | solution.py:154
  33.6 34.1 %collective-permute-start = (bf16[8,112,128]{2,1,0:T(8,128)(2,1)S(1)}, bf16[8,112,128]{2,1,0:T(8,128)(2,1)S(1)}, u32[]{:S(2)}, u32[]{:S(2)}) collective-permute-start(bf16[8,112,128]{2,1,0:T(8,128)(2,1)S(1)} %all-to-all-done), channel_id=1, source_target_pairs={{0,16},{16,32},{32,0},{1,17},{17,33},{33,1},{2,18},{18,34},{34,2},... | collective-permute-start | bytes 688136 | tf_op jit(solution)/shard_map/ppermute | solution.py:158
  41.5 26.1 %collective-permute-start.1 = (bf16[8,112,128]{2,1,0:T(8,128)(2,1)S(1)}, bf16[8,112,128]{2,1,0:T(8,128)(2,1)S(1)}, u32[]{:S(2)}, u32[]{:S(2)}) collective-permute-start(bf16[8,112,128]{2,1,0:T(8,128)(2,1)S(1)} %all-to-all-done), channel_id=1, source_target_pairs={{0,32},{16,0},{32,16},{1,33},{17,1},{33,17},{2,34},{18,2},{34,18},... | collective-permute-start | bytes 688136 | tf_op jit(solution)/shard_map/ppermute | solution.py:158
  55.2 23.3 %all-to-all-start.2 = ((f32[12,8,128]{2,1,0:T(8,128)}), f32[12,8,128]{2,1,0:T(8,128)S(1)}, u32[]{:S(2)}, u32[]{:S(2)}) async-start(f32[12,8,128]{2,1,0:T(8,128)} %shard_map.69), calls=%async_computation.2 | async-start | bytes 98304 | tf_op jit(solution)/shard_map/all_to_all | solution.py:154
  67.7 10.7 %copy-start.1 = (bf16[128,4608]{1,0:T(8,128)(2,1)S(1)}, bf16[128,4608]{1,0:T(8,128)(2,1)}, u32[]{:S(2)}) copy-start(bf16[128,4608]{1,0:T(8,128)(2,1)} %x_ref.3) | copy-start | bytes 3538948
  67.7 10.7 %copy-start.3 = (bf16[128,128]{1,0:T(8,128)(2,1)S(1)}, bf16[128,128]{1,0:T(8,128)(2,1)}, u32[]{:S(2)}) copy-start(bf16[128,128]{1,0:T(8,128)(2,1)} %cot_ref.3) | copy-start | bytes 98308
  67.8 10.7 %collective-permute-start.4 = (bf16[3,8,112,128]{3,2,1,0:T(8,128)(2,1)S(1)}, bf16[3,8,112,128]{3,2,1,0:T(8,128)(2,1)S(1)}, u32[]{:S(2)}, u32[]{:S(2)}) collective-permute-start(bf16[3,8,112,128]{3,2,1,0:T(8,128)(2,1)S(1)} %pad_maximum_fusion.own_ref), channel_id=1, source_target_pairs={{0,1},{1,0},{2,3},{3,2},{4,5},{5,4},{6,7},{7,6},{8,9},{9,8},{10,11... | collective-permute-start | bytes 2064392 | tf_op jit(solution)/shard_map/ppermute | solution.py:150

commit v4 on v3

--- a/solution.py
+++ b/solution.py
@@ -12,14 +12,30 @@
 TOK, D, H = 128, 4608, 128
 ROWS = D // DEVICES
 SHARD = D // (ZH * Y * C)
+
 SLAB = SHARD + 16
 HALF = D // C
 PART = HALF // PLANE
+PADDED = PART + 8
+SIDE = LINE * Y
 CHUNK = 512
 BF16, F16, F32 = jnp.bfloat16, jnp.float16, jnp.float32
 VMEM = pl.BlockSpec(memory_space=pltpu.VMEM)
 MIB = 1024 * 1024
 
+def make_slabs(w_ref, gain_ref, slabs_ref, gain_row, sem):
+    fetch = pltpu.make_async_copy(gain_ref, gain_row, sem.at[Y])
+    fetch.start()
+    copies = [pltpu.make_async_copy(w_ref, slabs_ref.at[y, :SHARD, :], sem.at[y]) for y in range(Y)]
+    for copy in copies:
+        copy.start()
+    fetch.wait()
+    gains = jnp.broadcast_to(gain_row[...].astype(F32), (16, SHARD)).astype(BF16)
+    for y in range(Y):
+        slabs_ref[y, SHARD:, :] = jnp.zeros((16, H), BF16)
+        slabs_ref[y, SHARD:, :SHARD] = gains
+    for copy in copies:
+        copy.wait()
 
 def inverse(ref):
     square = jnp.zeros((TOK, 128), F32)
@@ -27,7 +43,6 @@
         wide = ref[:, at : at + 128].astype(F32)
         square += wide * wide
     return lax.rsqrt(jnp.sum(square, axis=1, keepdims=True) * (1.0 / D) + EPS)
-
 
 def products(x_ref, scaled, all_ref):
     high = scaled.astype(BF16)
@@ -37,27 +52,15 @@
         pair = jnp.dot(x_ref[:, at : at + CHUNK].T, both, preferred_element_type=F32)
         all_ref[at : at + CHUNK, :] = pair[:, :H] + pair[:, H:]
 
-
-def rows_of(all_ref, chip, row, core, first, count):
-    start = chip // Y * (D // X) + chip % Y * (C * ROWS) + row + first * SHARD
-    return all_ref[pl.ds(start + core * ROWS, count, stride=SHARD), :]
-
-
-def pieces():
-    for row in range(ROWS):
-        for first, count in ((0, 8), (8, 4)) if row % 2 == 0 else ((0, 4), (4, 8)):
-            yield row, first, count, row * LINE + first
-
-
 def near_terms(x_ref, cot_ref, half_ref, inv_ref, all_ref):
     inv = inverse(x_ref)
     inv_ref[...] = jnp.broadcast_to(inv, (TOK, 128))
     products(x_ref, cot_ref[...].astype(F32) * inv, all_ref)
     mine = lax.axis_index("core")
-    for chip in range(PLANE):
-        for row, first, count, at in pieces():
-            half_ref[chip, at : at + count, :] = rows_of(all_ref, chip, row, mine, first, count)
-
+    for x in range(X):
+        for row in range(ROWS):
+            at = (x * ROWS + row) * SIDE
+            half_ref[at : at + SIDE, :] = all_ref[pl.ds(x * (D // X) + row + mine * ROWS, SIDE, stride=C * ROWS), :]
 
 def far_terms(x_ref, cot_ref, near_cot_ref, near_ref, half_ref, all_ref):
     cot = cot_ref[...].astype(F32)
@@ -66,12 +69,15 @@
     scale = jnp.exp2(-power)
     products(x_ref, cot * (inverse(x_ref) * scale), all_ref)
     mine = lax.axis_index("core")
+    for x in range(X):
+        for row in range(ROWS):
+            for place in range(LINE):
+                start = x * (D // X) + place * SHARD + row + mine * ROWS
+                at = (x * ROWS + row) * SIDE + place * Y
+                total = all_ref[pl.ds(start, Y, stride=C * ROWS), :] + near_ref[at : at + Y, :] * scale
+                half_ref[pl.ds(x * Y * PADDED + row * LINE + place, Y, stride=PADDED), :] = total
     for chip in range(PLANE):
-        for row, first, count, at in pieces():
-            to = slice(at, at + count)
-            half_ref[chip, to, :] = rows_of(all_ref, chip, row, mine, first, count) + near_ref[chip, to, :] * scale
-        half_ref[chip, PART:, :] = jnp.broadcast_to(power, (8, H))
-
+        half_ref[chip * PADDED + PART : (chip + 1) * PADDED, :] = jnp.broadcast_to(power, (8, H))
 
 def plane_sum(parts_ref, out_ref, sum_ref):
     total = jnp.zeros((PART, H), F32)
@@ -81,7 +87,6 @@
     sum_ref[PART:, :] = jnp.zeros((8 * LINE - PART, H), F32)
     for place in range(LINE):
         out_ref[place] = sum_ref[pl.ds(place, 8, stride=LINE), :]
-
 
 def outputs(x_ref, cot_ref, inv_ref, own_ref, other_ref, total_ref, grad_ref, weight_ref, gain_ref, w_ref, g_ref, sg_ref, win_ref):
     mine, my_y, my_zh = lax.axis_index("core"), lax.axis_index("y"), lax.axis_index("zh")
@@ -128,57 +133,59 @@
         normal = x_ref[:, here : here + 128].astype(F32) * inv
         grad_ref[:, here : here + 128] = (inv * (sg_ref[:, here : here + 128] - normal * mean)).astype(BF16)
 
-
 def last_sum(parts_ref, total_ref):
     total = parts_ref[0]
     for place in range(1, LINE):
         total += parts_ref[place]
     total_ref[...] = total * (1.0 / DEVICES)
 
-
-def call(body, outs, scratch=(), flops=0, moved=0):
+def call(body, outs, scratch=(), flops=0, moved=0, limit=40, **more):
     return pl.pallas_call(
         body,
+        **more,
         out_shape=[jax.ShapeDtypeStruct(*o) for o in outs],
         scratch_shapes=list(scratch),
-        compiler_params=pltpu.CompilerParams(vmem_limit_bytes=40 * MIB),
+        compiler_params=pltpu.CompilerParams(vmem_limit_bytes=limit * MIB),
         cost_estimate=pl.CostEstimate(flops=flops, bytes_accessed=moved, transcendentals=0),
     )
 
-
 def swap_cores(a):
     return lax.ppermute(a, "core", [(0, 1), (1, 0)])
 
-
 def exchange(a, axis):
     return lax.all_to_all(a, axis, split_axis=0, concat_axis=0, tiled=True)
 
-
 def shift(a, axis, n, by):
     return lax.ppermute(a, axis, [(i, (i + by) % n) for i in range(n)])
 
-
 def on_device(layer_input, norm_gain, kv_weight, kv_cotangent):
     far, far_cot = swap_cores(layer_input), swap_cores(kv_cotangent)
-    gains = jnp.broadcast_to(jnp.pad(norm_gain, (0, 128 - SHARD))[None], (16, 128))
-    slab = jnp.concatenate([kv_weight, gains], axis=0)
-    column = exchange(jnp.broadcast_to(slab[None], (Y, SLAB, H)), "y")
+    hbm = pl.BlockSpec(memory_space=pltpu.HBM)
+    (slabs,) = call(
+        make_slabs,
+        [((Y, SLAB, H), BF16)],
+        [pltpu.VMEM((1, SHARD), BF16), pltpu.SemaphoreType.DMA((Y + 1,))],
+        flops=int(2e10),
+        limit=60,
+        in_specs=[hbm, hbm],
+    )(kv_weight, norm_gain.reshape(1, SHARD))
+    column = exchange(slabs, "y")
     turns = [shift(column, "zh", ZH, turn) for turn in range(1, ZH)]
     near, inv = call(
         near_terms,
-        [((PLANE, PART, H), F32), ((TOK, 128), F32)],
+        [((HALF, H), F32), ((TOK, 128), F32)],
         [pltpu.VMEM((D, H), F32)],
         flops=4 * TOK * D * H,
         moved=2 * TOK * D + 2 * D * H,
     )(layer_input, kv_cotangent)
     (half,) = call(
         far_terms,
-        [((PLANE, PART + 8, H), F32)],
+        [((PLANE * PADDED, H), F32)],
         [pltpu.VMEM((D, H), F32)],
         flops=4 * TOK * D * H,
         moved=2 * TOK * D + 4 * D * H,
     )(far, far_cot, kv_cotangent, near)
-    parts = exchange(half.astype(F16), ("x", "y")).astype(F32)
+    parts = exchange(half.astype(F16).reshape(PLANE, PADDED, H), ("x", "y")).astype(F32)
     (sums,) = call(plane_sum, [((LINE, 8, H), F32)], [pltpu.VMEM((8 * LINE, H), F32)], flops=PLANE * PART * H, moved=4 * HALF * H)(parts)
     last = exchange(sums, ("zl", "zh"))
     turns, _ = lax.optimization_barrier((turns, sums))
@@ -199,7 +206,6 @@
         moved=4 * TOK * D,
     )(layer_input, kv_cotangent, inv, own, other, total)
 
-
 def solution(mesh):
     axes = ("x", "zl", "zh", "y", "core")
     fine = Mesh(mesh.devices.reshape(X, ZL, ZH, Y, C), axes)

time: 81.8 us -> 78.8 us (0.963)
  waiting for transfers between devices: 17.9 us -> 23.1 us
  starting transfers between devices: 50.2 us -> 45.6 us
  local copies, waits for them, and re-layouts: 3.42 us -> 0.01 us
    all_to_all x3, waiting for transfers between devices: 17.9 us -> 23.1 us  [exchange(): return lax.all_to_all(a, axis, split_axis=0, concat_axis=0, tiled=True)]
    all_to_all x3, starting transfers between devices: 30.6 us -> 27.8 us  [exchange(): return lax.all_to_all(a, axis, split_axis=0, concat_axis=0, tiled=True)]
    unnamed x8 -> x4, local copies, waits for them, and re-layouts: 2.04 us -> 0.01 us
    ppermute x2, starting transfers between devices: 13.5 us -> 11.9 us  [shift(): return lax.ppermute(a, axis, [(i, (i + by) % n) for i in range(n)])]
    pallas_call x2 -> x3, Pallas kernels: 3.62 us -> 4.33 us  [the longest x1 1.99 us: on_device(): call(make_slabs, [((Y, SLAB, H), BF16)], [pltpu.VMEM((1, SHARD), BF16), p...]
  transfers between devices with their start and end apart: 8 -> 8, of which waited for: 3 -> 3; matrix products, arithmetic and copies ran while one was open for 4% -> 1% of each run, Pallas kernels for 5% -> 6%
where the time goes in v4:
time: 78.8 us; the launch traced here: 78.3 us
  starting transfers between devices  45.6 us (58%)
  waiting for transfers between devices  23.1 us (29%)
  Pallas kernels  7.66 us (10%)
  other arithmetic  1.09 us (1%)
    all_to_all x3, starting transfers between devices, exchange(): return lax.all_to_all(a, axis, split_axis=0, concat_axis=0, tiled=True)  27.8 us
    all_to_all x3, waiting for transfers between devices, exchange(): return lax.all_to_all(a, axis, split_axis=0, concat_axis=0, tiled=True)  23.1 us
    ppermute x2, starting transfers between devices, shift(): return lax.ppermute(a, axis, [(i, (i + by) % n) for i in range(n)])  11.9 us
    ppermute x3, starting transfers between devices, swap_cores(): return lax.ppermute(a, 'core', [(0, 1), (1, 0)])  5.96 us
    pallas_call x1, Pallas kernels, on_device(): call(outputs, [((TOK, D), BF16), ((ROWS, H), F32), ((ROWS,), F32)], [pltp...  2.59 us
    pallas_call x1, Pallas kernels, on_device(): call(make_slabs, [((Y, SLAB, H), BF16)], [pltpu.VMEM((1, SHARD), BF16), p...  1.99 us
  transfers between devices with their start and end apart: 8, of which 3 were waited for; matrix products, arithmetic and copies ran while one was open for 1% of the time, Pallas kernels for 6%

profile of v4, /device:TPU:8, one launch (start us, length us, event | category | flops | bytes accessed | tf_op | source)
XLA Modules:
  0.0 78.3 jit_solution(14030361095584867140)
XLA Ops:
  0.6 1.9 %collective-permute-start.2 = (bf16[128,4608]{1,0:T(8,128)(2,1)}, bf16[128,4608]{1,0:T(8,128)(2,1)S(1)}, u32[]{:S(2)}, u32[]{:S(2)}) collective-permute-start(bf16[128,4608]{1,0:T(8,128)(2,1)} %x_ref.3), channel_id=1, source_target_pairs={{0,1},{1,0},{2,3},{3,2},{4,5},{5,4},{6,7},{7,6},{8,9},{9,8},{10,11... | collective-permute-start | bytes 3538952 | tf_op jit(solution)/shard_map/ppermute | solution.py:153
  2.6 0.0 copy-start.1
  2.6 0.0 copy-start
  2.6 2.0 %shard_map.68 = bf16[8,112,128]{2,1,0:T(8,128)(2,1)} custom-call(bf16[96,128]{1,0:T(8,128)(2,1)} %w_ref.1, bf16[1,96]{1,0:T(2,128)(2,1)} %bitcast.8), custom_call_target="tpu_custom_call" | custom-call | flops 20000000000 | tf_op jit(solution)/shard_map/pallas_call | solution.py:164
  4.6 12.8 %all-to-all-start = ((bf16[8,112,128]{2,1,0:T(8,128)(2,1)}), bf16[8,112,128]{2,1,0:T(8,128)(2,1)S(1)}, u32[]{:S(2)}, u32[]{:S(2)}) async-start(bf16[8,112,128]{2,1,0:T(8,128)(2,1)} %shard_map.68), calls=%async_computation | async-start | bytes 458752 | tf_op jit(solution)/shard_map/all_to_all | solution.py:156
  17.4 0.0 copy-done.1
  17.4 2.1 %collective-permute-start.3 = (bf16[128,128]{1,0:T(8,128)(2,1)S(1)}, bf16[128,128]{1,0:T(8,128)(2,1)S(1)}, u32[]{:S(2)}, u32[]{:S(2)}) collective-permute-start(bf16[128,128]{1,0:T(8,128)(2,1)S(1)} %copy-done.1), channel_id=1, source_target_pairs={{0,1},{1,0},{2,3},{3,2},{4,5},{5,4},{6,7},{7,6},{8,9},{9,8},{10,11... | collective-permute-start | bytes 98312 | tf_op jit(solution)/shard_map/ppermute | solution.py:153
  19.5 0.0 copy-done
  19.5 1.1 %shard_map.67 = (f32[2304,128]{1,0:T(8,128)S(1)}, f32[128,128]{1,0:T(8,128)S(1)}) custom-call(bf16[128,4608]{1,0:T(8,128)(2,1)S(1)} %copy-done, bf16[128,128]{1,0:T(8,128)(2,1)S(1)} %copy-done.1), custom_call_target="tpu_custom_call" | custom-call | flops 301989888 | bytes 2359296 | tf_op jit(solution)/shard_map/pallas_call | solution.py:174
  20.6 0.0 collective-permute-done.3.cot_ref
  20.6 0.0 collective-permute-done.2.x_ref
  20.6 1.3 %shard_map.69 = f32[2560,128]{1,0:T(8,128)S(1)} custom-call(bf16[128,4608]{1,0:T(8,128)(2,1)S(1)} %collective-permute-done.2.x_ref, bf16[128,128]{1,0:T(8,128)(2,1)S(1)} %collective-permute-done.3.cot_ref, bf16[128,128]{1,0:T(8,128)(2,1)S(1)} %copy-done.1, f32[2304,128]{1,0:T(8,128)S(1)} %get-tuple-element.8.near_ref), custom_call_target="tpu_custom_call" | custom-call | flops 301989888 | bytes 3538944 | tf_op jit(solution)/shard_map/pallas_call | solution.py:181
  21.9 0.9 %convert_element_type.6 = f16[2560,128]{1,0:T(8,128)(2,1)} convert(f32[2560,128]{1,0:T(8,128)S(1)} %shard_map.69) | non-fusion elementwise | flops 327680 | bytes 1966080 | tf_op jit(solution)/shard_map/convert_element_type | solution.py:188
  22.8 5.3 %all-to-all-done = bf16[8,112,128]{2,1,0:T(8,128)(2,1)S(1)} async-done(((bf16[8,112,128]{2,1,0:T(8,128)(2,1)}), bf16[8,112,128]{2,1,0:T(8,128)(2,1)S(1)}, u32[]{:S(2)}, u32[]{:S(2)}) %all-to-all-start) | async-done | bytes 229408 | tf_op jit(solution)/shard_map/all_to_all | solution.py:156
  28.0 5.0 %all-to-all-start.1 = ((f16[32,80,128]{2,1,0:T(8,128)(2,1)}), f16[32,80,128]{2,1,0:T(8,128)(2,1)S(1)}, u32[]{:S(2)}, u32[]{:S(2)}) async-start(f16[32,80,128]{2,1,0:T(8,128)(2,1)} %bitcast.2), calls=%async_computation.1 | async-start | bytes 1310720 | tf_op jit(solution)/shard_map/all_to_all | solution.py:156
  33.1 6.3 %collective-permute-start = (bf16[8,112,128]{2,1,0:T(8,128)(2,1)S(1)}, bf16[8,112,128]{2,1,0:T(8,128)(2,1)S(1)}, u32[]{:S(2)}, u32[]{:S(2)}) collective-permute-start(bf16[8,112,128]{2,1,0:T(8,128)(2,1)S(1)} %all-to-all-done), channel_id=1, source_target_pairs={{0,16},{16,32},{32,0},{1,17},{17,33},{33,1},{2,18},{18,34},{34,2},... | collective-permute-start | bytes 688136 | tf_op jit(solution)/shard_map/ppermute | solution.py:159
  39.4 5.6 %collective-permute-start.1 = (bf16[8,112,128]{2,1,0:T(8,128)(2,1)S(1)}, bf16[8,112,128]{2,1,0:T(8,128)(2,1)S(1)}, u32[]{:S(2)}, u32[]{:S(2)}) collective-permute-start(bf16[8,112,128]{2,1,0:T(8,128)(2,1)S(1)} %all-to-all-done), channel_id=1, source_target_pairs={{0,32},{16,0},{32,16},{1,33},{17,1},{33,17},{2,34},{18,2},{34,18},... | collective-permute-start | bytes 688136 | tf_op jit(solution)/shard_map/ppermute | solution.py:159
  44.9 9.1 %all-to-all-done.1 = f16[32,80,128]{2,1,0:T(8,128)(2,1)S(1)} async-done(((f16[32,80,128]{2,1,0:T(8,128)(2,1)}), f16[32,80,128]{2,1,0:T(8,128)(2,1)S(1)}, u32[]{:S(2)}, u32[]{:S(2)}) %all-to-all-start.1) | async-done | bytes 655392 | tf_op jit(solution)/shard_map/all_to_all | solution.py:156
  54.0 0.1 convert_element_type.7.parts_ref
  54.1 0.7 shard_map.70
  54.8 10.0 %all-to-all-start.2 = ((f32[12,8,128]{2,1,0:T(8,128)}), f32[12,8,128]{2,1,0:T(8,128)S(1)}, u32[]{:S(2)}, u32[]{:S(2)}) async-start(f32[12,8,128]{2,1,0:T(8,128)} %shard_map.70), calls=%async_computation.2 | async-start | bytes 98304 | tf_op jit(solution)/shard_map/all_to_all | solution.py:156
  64.9 0.0 collective-permute-done
  64.9 0.0 collective-permute-done.1
  64.9 0.1 pad_maximum_fusion.own_ref
  65.0 1.9 %collective-permute-start.4 = (bf16[3,8,112,128]{3,2,1,0:T(8,128)(2,1)S(1)}, bf16[3,8,112,128]{3,2,1,0:T(8,128)(2,1)S(1)}, u32[]{:S(2)}, u32[]{:S(2)}) collective-permute-start(bf16[3,8,112,128]{3,2,1,0:T(8,128)(2,1)S(1)} %pad_maximum_fusion.own_ref), channel_id=1, source_target_pairs={{0,1},{1,0},{2,3},{3,2},{4,5},{5,4},{6,7},{7,6},{8,9},{9,8},{10,11... | collective-permute-start | bytes 2064392 | tf_op jit(solution)/shard_map/ppermute | solution.py:153
  66.9 8.8 %all-to-all-done.2.parts_ref = f32[12,8,128]{2,1,0:T(8,128)S(1)} async-done(((f32[12,8,128]{2,1,0:T(8,128)}), f32[12,8,128]{2,1,0:T(8,128)S(1)}, u32[]{:S(2)}, u32[]{:S(2)}) %all-to-all-start.2) | async-done | bytes 49184 | tf_op jit(solution)/shard_map/all_to_all | solution.py:156
  75.7 0.0 collective-permute-done.4.other_ref
  75.7 2.6 %shard_map.72 = (bf16[128,4608]{1,0:T(8,128)(2,1)}, f32[6,128]{1,0:T(8,128)}, f32[6]{0:T(128)}) custom-call(bf16[128,4608]{1,0:T(8,128)(2,1)S(1)} %copy-done, bf16[128,128]{1,0:T(8,128)(2,1)S(1)} %copy-done.1, f32[128,128]{1,0:T(8,128)S(1)} %get-tuple-element.7.inv_ref, bf16[3,8,112,128]{3,2,1,0:T(8,128)(2,1)S(1)} %pad_maximum_fusion.own_ref, ...), custom_call_target="tpu_custom_call" | custom-call | flops 150994944 | bytes 2359296 | tf_op jit(solution)/shard_map/pallas_call | solution.py:196
  (1 shorter events, 0.0 us)
Async XLA Ops:
  0.6 20.0 %collective-permute-start.2 = (bf16[128,4608]{1,0:T(8,128)(2,1)}, bf16[128,4608]{1,0:T(8,128)(2,1)S(1)}, u32[]{:S(2)}, u32[]{:S(2)}) collective-permute-start(bf16[128,4608]{1,0:T(8,128)(2,1)} %x_ref.3), channel_id=1, source_target_pairs={{0,1},{1,0},{2,3},{3,2},{4,5},{5,4},{6,7},{7,6},{8,9},{9,8},{10,11... | collective-permute-start | bytes 3538952 | tf_op jit(solution)/shard_map/ppermute | solution.py:153
  2.6 14.8 %copy-start.1 = (bf16[128,128]{1,0:T(8,128)(2,1)S(1)}, bf16[128,128]{1,0:T(8,128)(2,1)}, u32[]{:S(2)}) copy-start(bf16[128,128]{1,0:T(8,128)(2,1)} %cot_ref.3) | copy-start | bytes 98308
  2.6 16.9 %copy-start = (bf16[128,4608]{1,0:T(8,128)(2,1)S(1)}, bf16[128,4608]{1,0:T(8,128)(2,1)}, u32[]{:S(2)}) copy-start(bf16[128,4608]{1,0:T(8,128)(2,1)} %x_ref.3) | copy-start | bytes 3538948
  4.6 23.5 %all-to-all-start = ((bf16[8,112,128]{2,1,0:T(8,128)(2,1)}), bf16[8,112,128]{2,1,0:T(8,128)(2,1)S(1)}, u32[]{:S(2)}, u32[]{:S(2)}) async-start(bf16[8,112,128]{2,1,0:T(8,128)(2,1)} %shard_map.68), calls=%async_computation | async-start | bytes 458752 | tf_op jit(solution)/shard_map/all_to_all | solution.py:156
  17.4 3.2 %collective-permute-start.3 = (bf16[128,128]{1,0:T(8,128)(2,1)S(1)}, bf16[128,128]{1,0:T(8,128)(2,1)S(1)}, u32[]{:S(2)}, u32[]{:S(2)}) collective-permute-start(bf16[128,128]{1,0:T(8,128)(2,1)S(1)} %copy-done.1), channel_id=1, source_target_pairs={{0,1},{1,0},{2,3},{3,2},{4,5},{5,4},{6,7},{7,6},{8,9},{9,8},{10,11... | collective-permute-start | bytes 98312 | tf_op jit(solution)/shard_map/ppermute | solution.py:153
  28.0 25.9 %all-to-all-start.1 = ((f16[32,80,128]{2,1,0:T(8,128)(2,1)}), f16[32,80,128]{2,1,0:T(8,128)(2,1)S(1)}, u32[]{:S(2)}, u32[]{:S(2)}) async-start(f16[32,80,128]{2,1,0:T(8,128)(2,1)} %bitcast.2), calls=%async_computation.1 | async-start | bytes 1310720 | tf_op jit(solution)/shard_map/all_to_all | solution.py:156
  33.1 31.8 %collective-permute-start = (bf16[8,112,128]{2,1,0:T(8,128)(2,1)S(1)}, bf16[8,112,128]{2,1,0:T(8,128)(2,1)S(1)}, u32[]{:S(2)}, u32[]{:S(2)}) collective-permute-start(bf16[8,112,128]{2,1,0:T(8,128)(2,1)S(1)} %all-to-all-done), channel_id=1, source_target_pairs={{0,16},{16,32},{32,0},{1,17},{17,33},{33,1},{2,18},{18,34},{34,2},... | collective-permute-start | bytes 688136 | tf_op jit(solution)/shard_map/ppermute | solution.py:159
  39.4 25.5 %collective-permute-start.1 = (bf16[8,112,128]{2,1,0:T(8,128)(2,1)S(1)}, bf16[8,112,128]{2,1,0:T(8,128)(2,1)S(1)}, u32[]{:S(2)}, u32[]{:S(2)}) collective-permute-start(bf16[8,112,128]{2,1,0:T(8,128)(2,1)S(1)} %all-to-all-done), channel_id=1, source_target_pairs={{0,32},{16,0},{32,16},{1,33},{17,1},{33,17},{2,34},{18,2},{34,18},... | collective-permute-start | bytes 688136 | tf_op jit(solution)/shard_map/ppermute | solution.py:159
  54.8 20.9 %all-to-all-start.2 = ((f32[12,8,128]{2,1,0:T(8,128)}), f32[12,8,128]{2,1,0:T(8,128)S(1)}, u32[]{:S(2)}, u32[]{:S(2)}) async-start(f32[12,8,128]{2,1,0:T(8,128)} %shard_map.70), calls=%async_computation.2 | async-start | bytes 98304 | tf_op jit(solution)/shard_map/all_to_all | solution.py:156
  65.0 10.7 %collective-permute-start.4 = (bf16[3,8,112,128]{3,2,1,0:T(8,128)(2,1)S(1)}, bf16[3,8,112,128]{3,2,1,0:T(8,128)(2,1)S(1)}, u32[]{:S(2)}, u32[]{:S(2)}) collective-permute-start(bf16[3,8,112,128]{3,2,1,0:T(8,128)(2,1)S(1)} %pad_maximum_fusion.own_ref), channel_id=1, source_target_pairs={{0,1},{1,0},{2,3},{3,2},{4,5},{5,4},{6,7},{7,6},{8,9},{9,8},{10,11... | collective-permute-start | bytes 2064392 | tf_op jit(solution)/shard_map/ppermute | solution.py:153

commit v5 on v4

--- a/solution.py
+++ b/solution.py
@@ -12,7 +12,6 @@
 TOK, D, H = 128, 4608, 128
 ROWS = D // DEVICES
 SHARD = D // (ZH * Y * C)
-
 SLAB = SHARD + 16
 HALF = D // C
 PART = HALF // PLANE
@@ -23,19 +22,23 @@
 VMEM = pl.BlockSpec(memory_space=pltpu.VMEM)
 MIB = 1024 * 1024
 
-def make_slabs(w_ref, gain_ref, slabs_ref, gain_row, sem):
-    fetch = pltpu.make_async_copy(gain_ref, gain_row, sem.at[Y])
-    fetch.start()
-    copies = [pltpu.make_async_copy(w_ref, slabs_ref.at[y, :SHARD, :], sem.at[y]) for y in range(Y)]
+def make_slabs(w_ref, gain_ref, slabs_ref, slab, gain_row, sem):
+    fetches = [
+        pltpu.make_async_copy(gain_ref, gain_row, sem.at[Y]),
+        pltpu.make_async_copy(w_ref, slab.at[:SHARD, :], sem.at[Y + 1]),
+    ]
+    for copy in fetches:
+        copy.start()
+    slab[SHARD:, :] = jnp.zeros((16, H), BF16)
+    fetches[0].wait()
+    slab[SHARD:, :SHARD] = jnp.broadcast_to(gain_row[...].astype(F32), (16, SHARD)).astype(BF16)
+    fetches[1].wait()
+    copies = [pltpu.make_async_copy(slab, slabs_ref.at[y], sem.at[y]) for y in range(Y)]
     for copy in copies:
         copy.start()
-    fetch.wait()
-    gains = jnp.broadcast_to(gain_row[...].astype(F32), (16, SHARD)).astype(BF16)
-    for y in range(Y):
-        slabs_ref[y, SHARD:, :] = jnp.zeros((16, H), BF16)
-        slabs_ref[y, SHARD:, :SHARD] = gains
     for copy in copies:
         copy.wait()
+
 
 def inverse(ref):
     square = jnp.zeros((TOK, 128), F32)
@@ -159,23 +162,25 @@
     return lax.ppermute(a, axis, [(i, (i + by) % n) for i in range(n)])
 
 def on_device(layer_input, norm_gain, kv_weight, kv_cotangent):
-    far, far_cot = swap_cores(layer_input), swap_cores(kv_cotangent)
     hbm = pl.BlockSpec(memory_space=pltpu.HBM)
     (slabs,) = call(
         make_slabs,
         [((Y, SLAB, H), BF16)],
-        [pltpu.VMEM((1, SHARD), BF16), pltpu.SemaphoreType.DMA((Y + 1,))],
+        [pltpu.VMEM((SLAB, H), BF16), pltpu.VMEM((1, SHARD), BF16), pltpu.SemaphoreType.DMA((Y + 2,))],
         flops=int(2e10),
         limit=60,
         in_specs=[hbm, hbm],
+        out_specs=[hbm],
     )(kv_weight, norm_gain.reshape(1, SHARD))
     column = exchange(slabs, "y")
+    _, rows, cotangent = lax.optimization_barrier((slabs, layer_input, kv_cotangent))
+    far, far_cot = swap_cores(rows), swap_cores(cotangent)
     turns = [shift(column, "zh", ZH, turn) for turn in range(1, ZH)]
     near, inv = call(
         near_terms,
         [((HALF, H), F32), ((TOK, 128), F32)],
         [pltpu.VMEM((D, H), F32)],
-        flops=4 * TOK * D * H,
+        flops=int(3e10),
         moved=2 * TOK * D + 2 * D * H,
     )(layer_input, kv_cotangent)
     (half,) = call(

time: 78.8 us -> 77.8 us (0.987)
  waiting for transfers between devices: 23.1 us -> 16.4 us
  starting transfers between devices: 45.6 us -> 51.7 us
    all_to_all x3, waiting for transfers between devices: 23.1 us -> 16.4 us  [exchange(): return lax.all_to_all(a, axis, split_axis=0, concat_axis=0, tiled=True)]
    all_to_all x3, starting transfers between devices: 27.8 us -> 31.8 us  [exchange(): return lax.all_to_all(a, axis, split_axis=0, concat_axis=0, tiled=True)]
    ppermute x2, starting transfers between devices: 11.9 us -> 13.7 us  [shift(): return lax.ppermute(a, axis, [(i, (i + by) % n) for i in range(n)])]
  transfers between devices with their start and end apart: 8 -> 8, of which waited for: 3 -> 3; matrix products, arithmetic and copies ran while one was open for 1% -> 1% of each run, Pallas kernels for 6% -> 4%
where the time goes in v5:
time: 77.8 us; the launch traced here: 77.3 us
  starting transfers between devices  51.7 us (66%)
  waiting for transfers between devices  16.4 us (21%)
  Pallas kernels  7.29 us (9%)
  other arithmetic  1.09 us (1%)
  between operations  0.78 us (1%)
    all_to_all x3, starting transfers between devices, exchange(): return lax.all_to_all(a, axis, split_axis=0, concat_axis=0, tiled=True)  31.8 us
    all_to_all x3, waiting for transfers between devices, exchange(): return lax.all_to_all(a, axis, split_axis=0, concat_axis=0, tiled=True)  16.4 us
    ppermute x2, starting transfers between devices, shift(): return lax.ppermute(a, axis, [(i, (i + by) % n) for i in range(n)])  13.7 us
    ppermute x3, starting transfers between devices, swap_cores(): return lax.ppermute(a, 'core', [(0, 1), (1, 0)])  6.24 us
    pallas_call x1, Pallas kernels, on_device(): call(outputs, [((TOK, D), BF16), ((ROWS, H), F32), ((ROWS,), F32)], [pltp...  2.58 us
    pallas_call x1, Pallas kernels, on_device(): call(make_slabs, [((Y, SLAB, H), BF16)], [pltpu.VMEM((SLAB, H), BF16), pl...  1.63 us
  transfers between devices with their start and end apart: 8, of which 3 were waited for; matrix products, arithmetic and copies ran while one was open for 1% of the time, Pallas kernels for 4%

profile of v5, /device:TPU:8, one launch (start us, length us, event | category | flops | bytes accessed | tf_op | source)
XLA Modules:
  0.0 77.3 jit_solution(15622379584706815810)
XLA Ops:
  0.6 0.0 copy-start
  0.6 0.0 copy-start.1
  0.7 1.6 %shard_map.68 = bf16[8,112,128]{2,1,0:T(8,128)(2,1)} custom-call(bf16[96,128]{1,0:T(8,128)(2,1)} %w_ref.1, bf16[1,96]{1,0:T(2,128)(2,1)} %bitcast.8), custom_call_target="tpu_custom_call" | custom-call | flops 20000000000 | tf_op jit(solution)/shard_map/pallas_call | solution.py:166
  2.3 12.8 %all-to-all-start = ((bf16[8,112,128]{2,1,0:T(8,128)(2,1)}), bf16[8,112,128]{2,1,0:T(8,128)(2,1)S(1)}, u32[]{:S(2)}, u32[]{:S(2)}) async-start(bf16[8,112,128]{2,1,0:T(8,128)(2,1)} %shard_map.68), calls=%async_computation | async-start | bytes 458752 | tf_op jit(solution)/shard_map/all_to_all | solution.py:159
  15.1 0.0 copy-done
  15.1 1.9 %collective-permute-start.2 = (bf16[128,4608]{1,0:T(8,128)(2,1)S(1)}, bf16[128,4608]{1,0:T(8,128)(2,1)S(1)}, u32[]{:S(2)}, u32[]{:S(2)}) collective-permute-start(bf16[128,4608]{1,0:T(8,128)(2,1)S(1)} %copy-done), channel_id=1, source_target_pairs={{0,1},{1,0},{2,3},{3,2},{4,5},{5,4},{6,7},{7,6},{8,9},{9,8},{10,11... | collective-permute-start | bytes 3538952 | tf_op jit(solution)/shard_map/ppermute | solution.py:156
  17.0 0.0 copy-done.1
  17.0 2.4 %collective-permute-start.3 = (bf16[128,128]{1,0:T(8,128)(2,1)S(1)}, bf16[128,128]{1,0:T(8,128)(2,1)S(1)}, u32[]{:S(2)}, u32[]{:S(2)}) collective-permute-start(bf16[128,128]{1,0:T(8,128)(2,1)S(1)} %copy-done.1), channel_id=1, source_target_pairs={{0,1},{1,0},{2,3},{3,2},{4,5},{5,4},{6,7},{7,6},{8,9},{9,8},{10,11... | collective-permute-start | bytes 98312 | tf_op jit(solution)/shard_map/ppermute | solution.py:156
  19.4 1.1 %shard_map.67 = (f32[2304,128]{1,0:T(8,128)S(1)}, f32[128,128]{1,0:T(8,128)S(1)}) custom-call(bf16[128,4608]{1,0:T(8,128)(2,1)S(1)} %copy-done, bf16[128,128]{1,0:T(8,128)(2,1)S(1)} %copy-done.1), custom_call_target="tpu_custom_call" | custom-call | flops 30000001024 | bytes 2359296 | tf_op jit(solution)/shard_map/pallas_call | solution.py:179
  20.5 0.0 collective-permute-done.3.cot_ref
  20.5 0.0 collective-permute-done.2.x_ref
  20.5 1.3 %shard_map.69 = f32[2560,128]{1,0:T(8,128)S(1)} custom-call(bf16[128,4608]{1,0:T(8,128)(2,1)S(1)} %collective-permute-done.2.x_ref, bf16[128,128]{1,0:T(8,128)(2,1)S(1)} %collective-permute-done.3.cot_ref, bf16[128,128]{1,0:T(8,128)(2,1)S(1)} %copy-done.1, f32[2304,128]{1,0:T(8,128)S(1)} %get-tuple-element.12.near_ref), custom_call_target="tpu_custom_call" | custom-call | flops 301989888 | bytes 3538944 | tf_op jit(solution)/shard_map/pallas_call | solution.py:186
  21.8 0.9 %convert_element_type.6 = f16[2560,128]{1,0:T(8,128)(2,1)} convert(f32[2560,128]{1,0:T(8,128)S(1)} %shard_map.69) | non-fusion elementwise | flops 327680 | bytes 1966080 | tf_op jit(solution)/shard_map/convert_element_type | solution.py:193
  22.7 0.8 %all-to-all-done = bf16[8,112,128]{2,1,0:T(8,128)(2,1)S(1)} async-done(((bf16[8,112,128]{2,1,0:T(8,128)(2,1)}), bf16[8,112,128]{2,1,0:T(8,128)(2,1)S(1)}, u32[]{:S(2)}, u32[]{:S(2)}) %all-to-all-start) | async-done | bytes 229408 | tf_op jit(solution)/shard_map/all_to_all | solution.py:159
  23.5 6.6 %all-to-all-start.1 = ((f16[32,80,128]{2,1,0:T(8,128)(2,1)}), f16[32,80,128]{2,1,0:T(8,128)(2,1)S(1)}, u32[]{:S(2)}, u32[]{:S(2)}) async-start(f16[32,80,128]{2,1,0:T(8,128)(2,1)} %bitcast.2), calls=%async_computation.1 | async-start | bytes 1310720 | tf_op jit(solution)/shard_map/all_to_all | solution.py:159
  30.1 8.1 %collective-permute-start = (bf16[8,112,128]{2,1,0:T(8,128)(2,1)S(1)}, bf16[8,112,128]{2,1,0:T(8,128)(2,1)S(1)}, u32[]{:S(2)}, u32[]{:S(2)}) collective-permute-start(bf16[8,112,128]{2,1,0:T(8,128)(2,1)S(1)} %all-to-all-done), channel_id=1, source_target_pairs={{0,16},{16,32},{32,0},{1,17},{17,33},{33,1},{2,18},{18,34},{34,2},... | collective-permute-start | bytes 688136 | tf_op jit(solution)/shard_map/ppermute | solution.py:162
  38.3 5.6 %collective-permute-start.1 = (bf16[8,112,128]{2,1,0:T(8,128)(2,1)S(1)}, bf16[8,112,128]{2,1,0:T(8,128)(2,1)S(1)}, u32[]{:S(2)}, u32[]{:S(2)}) collective-permute-start(bf16[8,112,128]{2,1,0:T(8,128)(2,1)S(1)} %all-to-all-done), channel_id=1, source_target_pairs={{0,32},{16,0},{32,16},{1,33},{17,1},{33,17},{2,34},{18,2},{34,18},... | collective-permute-start | bytes 688136 | tf_op jit(solution)/shard_map/ppermute | solution.py:162
  43.8 6.8 %all-to-all-done.1 = f16[32,80,128]{2,1,0:T(8,128)(2,1)S(1)} async-done(((f16[32,80,128]{2,1,0:T(8,128)(2,1)}), f16[32,80,128]{2,1,0:T(8,128)(2,1)S(1)}, u32[]{:S(2)}, u32[]{:S(2)}) %all-to-all-start.1) | async-done | bytes 655392 | tf_op jit(solution)/shard_map/all_to_all | solution.py:159
  50.6 0.1 convert_element_type.7.parts_ref
  50.7 0.7 shard_map.70
  51.4 12.4 %all-to-all-start.2 = ((f32[12,8,128]{2,1,0:T(8,128)}), f32[12,8,128]{2,1,0:T(8,128)S(1)}, u32[]{:S(2)}, u32[]{:S(2)}) async-start(f32[12,8,128]{2,1,0:T(8,128)} %shard_map.70), calls=%async_computation.2 | async-start | bytes 98304 | tf_op jit(solution)/shard_map/all_to_all | solution.py:159
  63.8 0.0 collective-permute-done
  63.8 0.0 collective-permute-done.1
  63.8 0.1 pad_maximum_fusion.own_ref
  63.9 1.9 %collective-permute-start.4 = (bf16[3,8,112,128]{3,2,1,0:T(8,128)(2,1)S(1)}, bf16[3,8,112,128]{3,2,1,0:T(8,128)(2,1)S(1)}, u32[]{:S(2)}, u32[]{:S(2)}) collective-permute-start(bf16[3,8,112,128]{3,2,1,0:T(8,128)(2,1)S(1)} %pad_maximum_fusion.own_ref), channel_id=1, source_target_pairs={{0,1},{1,0},{2,3},{3,2},{4,5},{5,4},{6,7},{7,6},{8,9},{9,8},{10,11... | collective-permute-start | bytes 2064392 | tf_op jit(solution)/shard_map/ppermute | solution.py:156
  65.9 8.8 %all-to-all-done.2.parts_ref = f32[12,8,128]{2,1,0:T(8,128)S(1)} async-done(((f32[12,8,128]{2,1,0:T(8,128)}), f32[12,8,128]{2,1,0:T(8,128)S(1)}, u32[]{:S(2)}, u32[]{:S(2)}) %all-to-all-start.2) | async-done | bytes 49184 | tf_op jit(solution)/shard_map/all_to_all | solution.py:159
  74.7 0.0 collective-permute-done.4.other_ref
  74.7 2.6 %shard_map.72 = (bf16[128,4608]{1,0:T(8,128)(2,1)}, f32[6,128]{1,0:T(8,128)}, f32[6]{0:T(128)}) custom-call(bf16[128,4608]{1,0:T(8,128)(2,1)S(1)} %copy-done, bf16[128,128]{1,0:T(8,128)(2,1)S(1)} %copy-done.1, f32[128,128]{1,0:T(8,128)S(1)} %get-tuple-element.9.inv_ref, bf16[3,8,112,128]{3,2,1,0:T(8,128)(2,1)S(1)} %pad_maximum_fusion.own_ref, ...), custom_call_target="tpu_custom_call" | custom-call | flops 150994944 | bytes 2359296 | tf_op jit(solution)/shard_map/pallas_call | solution.py:201
  (1 shorter events, 0.0 us)
Async XLA Ops:
  0.6 14.4 %copy-start = (bf16[128,4608]{1,0:T(8,128)(2,1)S(1)}, bf16[128,4608]{1,0:T(8,128)(2,1)}, u32[]{:S(2)}) copy-start(bf16[128,4608]{1,0:T(8,128)(2,1)} %x_ref.3) | copy-start | bytes 3538948
  0.6 16.3 %copy-start.1 = (bf16[128,128]{1,0:T(8,128)(2,1)S(1)}, bf16[128,128]{1,0:T(8,128)(2,1)}, u32[]{:S(2)}) copy-start(bf16[128,128]{1,0:T(8,128)(2,1)} %cot_ref.3) | copy-start | bytes 98308
  2.3 21.2 %all-to-all-start = ((bf16[8,112,128]{2,1,0:T(8,128)(2,1)}), bf16[8,112,128]{2,1,0:T(8,128)(2,1)S(1)}, u32[]{:S(2)}, u32[]{:S(2)}) async-start(bf16[8,112,128]{2,1,0:T(8,128)(2,1)} %shard_map.68), calls=%async_computation | async-start | bytes 458752 | tf_op jit(solution)/shard_map/all_to_all | solution.py:159
  15.1 5.4 %collective-permute-start.2 = (bf16[128,4608]{1,0:T(8,128)(2,1)S(1)}, bf16[128,4608]{1,0:T(8,128)(2,1)S(1)}, u32[]{:S(2)}, u32[]{:S(2)}) collective-permute-start(bf16[128,4608]{1,0:T(8,128)(2,1)S(1)} %copy-done), channel_id=1, source_target_pairs={{0,1},{1,0},{2,3},{3,2},{4,5},{5,4},{6,7},{7,6},{8,9},{9,8},{10,11... | collective-permute-start | bytes 3538952 | tf_op jit(solution)/shard_map/ppermute | solution.py:156
  17.0 3.5 %collective-permute-start.3 = (bf16[128,128]{1,0:T(8,128)(2,1)S(1)}, bf16[128,128]{1,0:T(8,128)(2,1)S(1)}, u32[]{:S(2)}, u32[]{:S(2)}) collective-permute-start(bf16[128,128]{1,0:T(8,128)(2,1)S(1)} %copy-done.1), channel_id=1, source_target_pairs={{0,1},{1,0},{2,3},{3,2},{4,5},{5,4},{6,7},{7,6},{8,9},{9,8},{10,11... | collective-permute-start | bytes 98312 | tf_op jit(solution)/shard_map/ppermute | solution.py:156
  23.5 27.1 %all-to-all-start.1 = ((f16[32,80,128]{2,1,0:T(8,128)(2,1)}), f16[32,80,128]{2,1,0:T(8,128)(2,1)S(1)}, u32[]{:S(2)}, u32[]{:S(2)}) async-start(f16[32,80,128]{2,1,0:T(8,128)(2,1)} %bitcast.2), calls=%async_computation.1 | async-start | bytes 1310720 | tf_op jit(solution)/shard_map/all_to_all | solution.py:159
  30.1 33.7 %collective-permute-start = (bf16[8,112,128]{2,1,0:T(8,128)(2,1)S(1)}, bf16[8,112,128]{2,1,0:T(8,128)(2,1)S(1)}, u32[]{:S(2)}, u32[]{:S(2)}) collective-permute-start(bf16[8,112,128]{2,1,0:T(8,128)(2,1)S(1)} %all-to-all-done), channel_id=1, source_target_pairs={{0,16},{16,32},{32,0},{1,17},{17,33},{33,1},{2,18},{18,34},{34,2},... | collective-permute-start | bytes 688136 | tf_op jit(solution)/shard_map/ppermute | solution.py:162
  38.3 25.6 %collective-permute-start.1 = (bf16[8,112,128]{2,1,0:T(8,128)(2,1)S(1)}, bf16[8,112,128]{2,1,0:T(8,128)(2,1)S(1)}, u32[]{:S(2)}, u32[]{:S(2)}) collective-permute-start(bf16[8,112,128]{2,1,0:T(8,128)(2,1)S(1)} %all-to-all-done), channel_id=1, source_target_pairs={{0,32},{16,0},{32,16},{1,33},{17,1},{33,17},{2,34},{18,2},{34,18},... | collective-permute-start | bytes 688136 | tf_op jit(solution)/shard_map/ppermute | solution.py:162
  51.4 23.2 %all-to-all-start.2 = ((f32[12,8,128]{2,1,0:T(8,128)}), f32[12,8,128]{2,1,0:T(8,128)S(1)}, u32[]{:S(2)}, u32[]{:S(2)}) async-start(f32[12,8,128]{2,1,0:T(8,128)} %shard_map.70), calls=%async_computation.2 | async-start | bytes 98304 | tf_op jit(solution)/shard_map/all_to_all | solution.py:159
  63.9 10.7 %collective-permute-start.4 = (bf16[3,8,112,128]{3,2,1,0:T(8,128)(2,1)S(1)}, bf16[3,8,112,128]{3,2,1,0:T(8,128)(2,1)S(1)}, u32[]{:S(2)}, u32[]{:S(2)}) collective-permute-start(bf16[3,8,112,128]{3,2,1,0:T(8,128)(2,1)S(1)} %pad_maximum_fusion.own_ref), channel_id=1, source_target_pairs={{0,1},{1,0},{2,3},{3,2},{4,5},{5,4},{6,7},{7,6},{8,9},{9,8},{10,11... | collective-permute-start | bytes 2064392 | tf_op jit(solution)/shard_map/ppermute | solution.py:156

commit v6 on v5

--- a/solution.py
+++ b/solution.py
@@ -47,40 +47,33 @@
         square += wide * wide
     return lax.rsqrt(jnp.sum(square, axis=1, keepdims=True) * (1.0 / D) + EPS)
 
-def products(x_ref, scaled, all_ref):
+def row_scales(x_ref, inv_ref):
+    inv_ref[...] = jnp.broadcast_to(inverse(x_ref), (TOK, 128))
+
+
+def row_terms(x_ref, far_ref, cot_ref, far_cot_ref, inv_ref, half_ref, all_ref):
+    near, far = cot_ref[...].astype(F32), far_cot_ref[...].astype(F32)
+    largest = jnp.max(jnp.maximum(jnp.abs(near), jnp.abs(far)), axis=(0, 1), keepdims=True)
+    power = jnp.ceil(jnp.log2(jnp.maximum(largest, 1e-30)))
+    scale = jnp.exp2(-power)
+    scaled = jnp.concatenate([near * (inv_ref[...] * scale), far * (inverse(far_ref) * scale)], axis=0)
     high = scaled.astype(BF16)
     low = (scaled - high.astype(F32)).astype(BF16)
-    both = jnp.concatenate([high, low], axis=1)
+    parts = jnp.concatenate([high, low], axis=1)
     for at in range(0, D, CHUNK):
-        pair = jnp.dot(x_ref[:, at : at + CHUNK].T, both, preferred_element_type=F32)
+        turned = jnp.concatenate([x_ref[:, at : at + CHUNK].T, far_ref[:, at : at + CHUNK].T], axis=1)
+        pair = jnp.dot(turned, parts, preferred_element_type=F32)
         all_ref[at : at + CHUNK, :] = pair[:, :H] + pair[:, H:]
-
-def near_terms(x_ref, cot_ref, half_ref, inv_ref, all_ref):
-    inv = inverse(x_ref)
-    inv_ref[...] = jnp.broadcast_to(inv, (TOK, 128))
-    products(x_ref, cot_ref[...].astype(F32) * inv, all_ref)
-    mine = lax.axis_index("core")
-    for x in range(X):
-        for row in range(ROWS):
-            at = (x * ROWS + row) * SIDE
-            half_ref[at : at + SIDE, :] = all_ref[pl.ds(x * (D // X) + row + mine * ROWS, SIDE, stride=C * ROWS), :]
-
-def far_terms(x_ref, cot_ref, near_cot_ref, near_ref, half_ref, all_ref):
-    cot = cot_ref[...].astype(F32)
-    largest = jnp.max(jnp.maximum(jnp.abs(cot), jnp.abs(near_cot_ref[...].astype(F32))), axis=(0, 1), keepdims=True)
-    power = jnp.ceil(jnp.log2(jnp.maximum(largest, 1e-30)))
-    scale = jnp.exp2(-power)
-    products(x_ref, cot * (inverse(x_ref) * scale), all_ref)
     mine = lax.axis_index("core")
     for x in range(X):
         for row in range(ROWS):
             for place in range(LINE):
                 start = x * (D // X) + place * SHARD + row + mine * ROWS
-                at = (x * ROWS + row) * SIDE + place * Y
-                total = all_ref[pl.ds(start, Y, stride=C * ROWS), :] + near_ref[at : at + Y, :] * scale
-                half_ref[pl.ds(x * Y * PADDED + row * LINE + place, Y, stride=PADDED), :] = total
+                to = pl.ds(x * Y * PADDED + row * LINE + place, Y, stride=PADDED)
+                half_ref[to, :] = all_ref[pl.ds(start, Y, stride=C * ROWS), :]
     for chip in range(PLANE):
         half_ref[chip * PADDED + PART : (chip + 1) * PADDED, :] = jnp.broadcast_to(power, (8, H))
+
 
 def plane_sum(parts_ref, out_ref, sum_ref):
     total = jnp.zeros((PART, H), F32)
@@ -127,14 +120,15 @@
             found += jnp.where(column + here == wanted, gain, 0.0)
             scaled = grad[:, tile * 128 : tile * 128 + 128] * gain
             sg_ref[:, here : here + 128] = scaled
-            centre += scaled * (x_ref[:, here : here + 128].astype(F32) * inv)
+            centre += scaled * x_ref[:, here : here + 128].astype(F32)
     total = total_ref[...]
     weight_ref[...] = (total * jnp.sum(found, axis=1, keepdims=True))[:ROWS]
     gain_ref[...] = jnp.sum((total * win_ref[pl.ds(first - base, 8), :]).T, axis=0)[:ROWS]
-    mean = jnp.broadcast_to(jnp.sum(centre, axis=1, keepdims=True) * (1.0 / D), (TOK, 128))
+    pull = inv * inv * inv * (jnp.sum(centre, axis=1, keepdims=True) * (1.0 / D))
     for here in range(0, D, 128):
-        normal = x_ref[:, here : here + 128].astype(F32) * inv
-        grad_ref[:, here : here + 128] = (inv * (sg_ref[:, here : here + 128] - normal * mean)).astype(BF16)
+        wide = x_ref[:, here : here + 128].astype(F32)
+        grad_ref[:, here : here + 128] = (inv * sg_ref[:, here : here + 128] - wide * pull).astype(BF16)
+
 
 def last_sum(parts_ref, total_ref):
     total = parts_ref[0]
@@ -176,20 +170,8 @@
     _, rows, cotangent = lax.optimization_barrier((slabs, layer_input, kv_cotangent))
     far, far_cot = swap_cores(rows), swap_cores(cotangent)
     turns = [shift(column, "zh", ZH, turn) for turn in range(1, ZH)]
-    near, inv = call(
-        near_terms,
-        [((HALF, H), F32), ((TOK, 128), F32)],
-        [pltpu.VMEM((D, H), F32)],
-        flops=int(3e10),
-        moved=2 * TOK * D + 2 * D * H,
-    )(layer_input, kv_cotangent)
-    (half,) = call(
-        far_terms,
-        [((PLANE * PADDED, H), F32)],
-        [pltpu.VMEM((D, H), F32)],
-        flops=4 * TOK * D * H,
-        moved=2 * TOK * D + 4 * D * H,
-    )(far, far_cot, kv_cotangent, near)
+    (inv,) = call(row_scales, [((TOK, 128), F32)], flops=int(3e10))(layer_input)
+    (half,) = call(row_terms, [((PLANE * PADDED, H), F32)], [pltpu.VMEM((D, H), F32)])(layer_input, far, kv_cotangent, far_cot, inv)
     parts = exchange(half.astype(F16).reshape(PLANE, PADDED, H), ("x", "y")).astype(F32)
     (sums,) = call(plane_sum, [((LINE, 8, H), F32)], [pltpu.VMEM((8 * LINE, H), F32)], flops=PLANE * PART * H, moved=4 * HALF * H)(parts)
     last = exchange(sums, ("zl", "zh"))

time: 77.8 us -> 77.8 us (level)
  waiting for transfers between devices: 16.4 us -> 17.4 us
  Pallas kernels: 7.29 us -> 6.44 us
  transfers between devices with their start and end apart: 8 -> 8, of which waited for: 3 -> 4; matrix products, arithmetic and copies ran while one was open for 1% -> 1% of each run, Pallas kernels for 4% -> 3%
where the time goes in v6:
time: 77.8 us; the launch traced here: 77.3 us
  starting transfers between devices  51.5 us (66%)
  waiting for transfers between devices  17.4 us (22%)
  Pallas kernels  6.44 us (8%)
  other arithmetic  1.09 us (1%)
    all_to_all x3, starting transfers between devices, exchange(): return lax.all_to_all(a, axis, split_axis=0, concat_axis=0, tiled=True)  31.6 us
    all_to_all x3, waiting for transfers between devices, exchange(): return lax.all_to_all(a, axis, split_axis=0, concat_axis=0, tiled=True)  16.9 us
    ppermute x2, starting transfers between devices, shift(): return lax.ppermute(a, axis, [(i, (i + by) % n) for i in range(n)])  13.7 us
    ppermute x3, starting transfers between devices, swap_cores(): return lax.ppermute(a, 'core', [(0, 1), (1, 0)])  6.24 us
    pallas_call x1, Pallas kernels, on_device(): call(outputs, [((TOK, D), BF16), ((ROWS, H), F32), ((ROWS,), F32)], [pltp...  2.41 us
    pallas_call x1, Pallas kernels, on_device(): call(make_slabs, [((Y, SLAB, H), BF16)], [pltpu.VMEM((SLAB, H), BF16), pl...  1.64 us
  transfers between devices with their start and end apart: 8, of which 4 were waited for; matrix products, arithmetic and copies ran while one was open for 1% of the time, Pallas kernels for 3%

profile of v6, /device:TPU:8, one launch (start us, length us, event | category | flops | bytes accessed | tf_op | source)
XLA Modules:
  0.0 77.3 jit_solution(15320639121276049459)
XLA Ops:
  0.6 0.0 copy-start
  0.6 0.0 copy-start.1
  0.7 1.6 %shard_map.68 = bf16[8,112,128]{2,1,0:T(8,128)(2,1)} custom-call(bf16[96,128]{1,0:T(8,128)(2,1)} %w_ref.1, bf16[1,96]{1,0:T(2,128)(2,1)} %bitcast.8), custom_call_target="tpu_custom_call" | custom-call | flops 20000000000 | tf_op jit(solution)/shard_map/pallas_call | solution.py:160
  2.3 12.8 %all-to-all-start = ((bf16[8,112,128]{2,1,0:T(8,128)(2,1)}), bf16[8,112,128]{2,1,0:T(8,128)(2,1)S(1)}, u32[]{:S(2)}, u32[]{:S(2)}) async-start(bf16[8,112,128]{2,1,0:T(8,128)(2,1)} %shard_map.68), calls=%async_computation | async-start | bytes 458752 | tf_op jit(solution)/shard_map/all_to_all | solution.py:153
  15.1 0.0 copy-done
  15.1 1.9 %collective-permute-start.2 = (bf16[128,4608]{1,0:T(8,128)(2,1)S(1)}, bf16[128,4608]{1,0:T(8,128)(2,1)S(1)}, u32[]{:S(2)}, u32[]{:S(2)}) collective-permute-start(bf16[128,4608]{1,0:T(8,128)(2,1)S(1)} %copy-done), channel_id=1, source_target_pairs={{0,1},{1,0},{2,3},{3,2},{4,5},{5,4},{6,7},{7,6},{8,9},{9,8},{10,11... | collective-permute-start | bytes 3538952 | tf_op jit(solution)/shard_map/ppermute | solution.py:150
  17.0 0.0 copy-done.1
  17.0 2.4 %collective-permute-start.3 = (bf16[128,128]{1,0:T(8,128)(2,1)S(1)}, bf16[128,128]{1,0:T(8,128)(2,1)S(1)}, u32[]{:S(2)}, u32[]{:S(2)}) collective-permute-start(bf16[128,128]{1,0:T(8,128)(2,1)S(1)} %copy-done.1), channel_id=1, source_target_pairs={{0,1},{1,0},{2,3},{3,2},{4,5},{5,4},{6,7},{7,6},{8,9},{9,8},{10,11... | collective-permute-start | bytes 98312 | tf_op jit(solution)/shard_map/ppermute | solution.py:150
  19.4 0.3 shard_map.67.inv_ref
  19.7 0.5 collective-permute-done.3.far_cot_ref
  20.3 0.0 collective-permute-done.2.far_ref
  20.3 1.4 %shard_map.69 = f32[2560,128]{1,0:T(8,128)S(1)} custom-call(bf16[128,4608]{1,0:T(8,128)(2,1)S(1)} %copy-done, bf16[128,4608]{1,0:T(8,128)(2,1)S(1)} %collective-permute-done.2.far_ref, bf16[128,128]{1,0:T(8,128)(2,1)S(1)} %copy-done.1, bf16[128,128]{1,0:T(8,128)(2,1)S(1)} %collective-permute-done.3.far_cot_ref, f32[128,128]{1,0:T(8,128)S(1)} %shard_map.67.inv_ref), custom_call_target="tpu_custom_call" | custom-call | tf_op jit(solution)/shard_map/pallas_call | solution.py:174
  21.6 0.9 %convert_element_type.6 = f16[2560,128]{1,0:T(8,128)(2,1)} convert(f32[2560,128]{1,0:T(8,128)S(1)} %shard_map.69) | non-fusion elementwise | flops 327680 | bytes 1966080 | tf_op jit(solution)/shard_map/convert_element_type | solution.py:175
  22.5 1.0 %all-to-all-done = bf16[8,112,128]{2,1,0:T(8,128)(2,1)S(1)} async-done(((bf16[8,112,128]{2,1,0:T(8,128)(2,1)}), bf16[8,112,128]{2,1,0:T(8,128)(2,1)S(1)}, u32[]{:S(2)}, u32[]{:S(2)}) %all-to-all-start) | async-done | bytes 229408 | tf_op jit(solution)/shard_map/all_to_all | solution.py:153
  23.5 6.4 %all-to-all-start.1 = ((f16[32,80,128]{2,1,0:T(8,128)(2,1)}), f16[32,80,128]{2,1,0:T(8,128)(2,1)S(1)}, u32[]{:S(2)}, u32[]{:S(2)}) async-start(f16[32,80,128]{2,1,0:T(8,128)(2,1)} %bitcast.2), calls=%async_computation.1 | async-start | bytes 1310720 | tf_op jit(solution)/shard_map/all_to_all | solution.py:153
  29.9 8.1 %collective-permute-start = (bf16[8,112,128]{2,1,0:T(8,128)(2,1)S(1)}, bf16[8,112,128]{2,1,0:T(8,128)(2,1)S(1)}, u32[]{:S(2)}, u32[]{:S(2)}) collective-permute-start(bf16[8,112,128]{2,1,0:T(8,128)(2,1)S(1)} %all-to-all-done), channel_id=1, source_target_pairs={{0,16},{16,32},{32,0},{1,17},{17,33},{33,1},{2,18},{18,34},{34,2},... | collective-permute-start | bytes 688136 | tf_op jit(solution)/shard_map/ppermute | solution.py:156
  38.1 5.6 %collective-permute-start.1 = (bf16[8,112,128]{2,1,0:T(8,128)(2,1)S(1)}, bf16[8,112,128]{2,1,0:T(8,128)(2,1)S(1)}, u32[]{:S(2)}, u32[]{:S(2)}) collective-permute-start(bf16[8,112,128]{2,1,0:T(8,128)(2,1)S(1)} %all-to-all-done), channel_id=1, source_target_pairs={{0,32},{16,0},{32,16},{1,33},{17,1},{33,17},{2,34},{18,2},{34,18},... | collective-permute-start | bytes 688136 | tf_op jit(solution)/shard_map/ppermute | solution.py:156
  43.7 7.1 %all-to-all-done.1 = f16[32,80,128]{2,1,0:T(8,128)(2,1)S(1)} async-done(((f16[32,80,128]{2,1,0:T(8,128)(2,1)}), f16[32,80,128]{2,1,0:T(8,128)(2,1)S(1)}, u32[]{:S(2)}, u32[]{:S(2)}) %all-to-all-start.1) | async-done | bytes 655392 | tf_op jit(solution)/shard_map/all_to_all | solution.py:153
  50.8 0.1 convert_element_type.7.parts_ref
  50.9 0.7 shard_map.70
  51.6 12.4 %all-to-all-start.2 = ((f32[12,8,128]{2,1,0:T(8,128)}), f32[12,8,128]{2,1,0:T(8,128)S(1)}, u32[]{:S(2)}, u32[]{:S(2)}) async-start(f32[12,8,128]{2,1,0:T(8,128)} %shard_map.70), calls=%async_computation.2 | async-start | bytes 98304 | tf_op jit(solution)/shard_map/all_to_all | solution.py:153
  64.0 0.0 collective-permute-done
  64.0 0.0 collective-permute-done.1
  64.0 0.1 pad_maximum_fusion.own_ref
  64.1 1.9 %collective-permute-start.4 = (bf16[3,8,112,128]{3,2,1,0:T(8,128)(2,1)S(1)}, bf16[3,8,112,128]{3,2,1,0:T(8,128)(2,1)S(1)}, u32[]{:S(2)}, u32[]{:S(2)}) collective-permute-start(bf16[3,8,112,128]{3,2,1,0:T(8,128)(2,1)S(1)} %pad_maximum_fusion.own_ref), channel_id=1, source_target_pairs={{0,1},{1,0},{2,3},{3,2},{4,5},{5,4},{6,7},{7,6},{8,9},{9,8},{10,11... | collective-permute-start | bytes 2064392 | tf_op jit(solution)/shard_map/ppermute | solution.py:150
  66.0 8.8 %all-to-all-done.2.parts_ref = f32[12,8,128]{2,1,0:T(8,128)S(1)} async-done(((f32[12,8,128]{2,1,0:T(8,128)}), f32[12,8,128]{2,1,0:T(8,128)S(1)}, u32[]{:S(2)}, u32[]{:S(2)}) %all-to-all-start.2) | async-done | bytes 49184 | tf_op jit(solution)/shard_map/all_to_all | solution.py:153
  74.8 0.0 collective-permute-done.4.other_ref
  74.9 2.4 %shard_map.72 = (bf16[128,4608]{1,0:T(8,128)(2,1)}, f32[6,128]{1,0:T(8,128)}, f32[6]{0:T(128)}) custom-call(bf16[128,4608]{1,0:T(8,128)(2,1)S(1)} %copy-done, bf16[128,128]{1,0:T(8,128)(2,1)S(1)} %copy-done.1, f32[128,128]{1,0:T(8,128)S(1)} %shard_map.67.inv_ref, bf16[3,8,112,128]{3,2,1,0:T(8,128)(2,1)S(1)} %pad_maximum_fusion.own_ref, ...), custom_call_target="tpu_custom_call" | custom-call | flops 150994944 | bytes 2359296 | tf_op jit(solution)/shard_map/pallas_call | solution.py:183
  (1 shorter events, 0.0 us)
Async XLA Ops:
  0.6 14.4 %copy-start = (bf16[128,4608]{1,0:T(8,128)(2,1)S(1)}, bf16[128,4608]{1,0:T(8,128)(2,1)}, u32[]{:S(2)}) copy-start(bf16[128,4608]{1,0:T(8,128)(2,1)} %x_ref.5) | copy-start | bytes 3538948
  0.6 16.4 %copy-start.1 = (bf16[128,128]{1,0:T(8,128)(2,1)S(1)}, bf16[128,128]{1,0:T(8,128)(2,1)}, u32[]{:S(2)}) copy-start(bf16[128,128]{1,0:T(8,128)(2,1)} %cot_ref.3) | copy-start | bytes 98308
  2.3 21.2 %all-to-all-start = ((bf16[8,112,128]{2,1,0:T(8,128)(2,1)}), bf16[8,112,128]{2,1,0:T(8,128)(2,1)S(1)}, u32[]{:S(2)}, u32[]{:S(2)}) async-start(bf16[8,112,128]{2,1,0:T(8,128)(2,1)} %shard_map.68), calls=%async_computation | async-start | bytes 458752 | tf_op jit(solution)/shard_map/all_to_all | solution.py:153
  15.1 5.2 %collective-permute-start.2 = (bf16[128,4608]{1,0:T(8,128)(2,1)S(1)}, bf16[128,4608]{1,0:T(8,128)(2,1)S(1)}, u32[]{:S(2)}, u32[]{:S(2)}) collective-permute-start(bf16[128,4608]{1,0:T(8,128)(2,1)S(1)} %copy-done), channel_id=1, source_target_pairs={{0,1},{1,0},{2,3},{3,2},{4,5},{5,4},{6,7},{7,6},{8,9},{9,8},{10,11... | collective-permute-start | bytes 3538952 | tf_op jit(solution)/shard_map/ppermute | solution.py:150
  17.0 3.3 %collective-permute-start.3 = (bf16[128,128]{1,0:T(8,128)(2,1)S(1)}, bf16[128,128]{1,0:T(8,128)(2,1)S(1)}, u32[]{:S(2)}, u32[]{:S(2)}) collective-permute-start(bf16[128,128]{1,0:T(8,128)(2,1)S(1)} %copy-done.1), channel_id=1, source_target_pairs={{0,1},{1,0},{2,3},{3,2},{4,5},{5,4},{6,7},{7,6},{8,9},{9,8},{10,11... | collective-permute-start | bytes 98312 | tf_op jit(solution)/shard_map/ppermute | solution.py:150
  23.5 27.3 %all-to-all-start.1 = ((f16[32,80,128]{2,1,0:T(8,128)(2,1)}), f16[32,80,128]{2,1,0:T(8,128)(2,1)S(1)}, u32[]{:S(2)}, u32[]{:S(2)}) async-start(f16[32,80,128]{2,1,0:T(8,128)(2,1)} %bitcast.2), calls=%async_computation.1 | async-start | bytes 1310720 | tf_op jit(solution)/shard_map/all_to_all | solution.py:153
  29.9 34.1 %collective-permute-start = (bf16[8,112,128]{2,1,0:T(8,128)(2,1)S(1)}, bf16[8,112,128]{2,1,0:T(8,128)(2,1)S(1)}, u32[]{:S(2)}, u32[]{:S(2)}) collective-permute-start(bf16[8,112,128]{2,1,0:T(8,128)(2,1)S(1)} %all-to-all-done), channel_id=1, source_target_pairs={{0,16},{16,32},{32,0},{1,17},{17,33},{33,1},{2,18},{18,34},{34,2},... | collective-permute-start | bytes 688136 | tf_op jit(solution)/shard_map/ppermute | solution.py:156
  38.1 25.9 %collective-permute-start.1 = (bf16[8,112,128]{2,1,0:T(8,128)(2,1)S(1)}, bf16[8,112,128]{2,1,0:T(8,128)(2,1)S(1)}, u32[]{:S(2)}, u32[]{:S(2)}) collective-permute-start(bf16[8,112,128]{2,1,0:T(8,128)(2,1)S(1)} %all-to-all-done), channel_id=1, source_target_pairs={{0,32},{16,0},{32,16},{1,33},{17,1},{33,17},{2,34},{18,2},{34,18},... | collective-permute-start | bytes 688136 | tf_op jit(solution)/shard_map/ppermute | solution.py:156
  51.6 23.2 %all-to-all-start.2 = ((f32[12,8,128]{2,1,0:T(8,128)}), f32[12,8,128]{2,1,0:T(8,128)S(1)}, u32[]{:S(2)}, u32[]{:S(2)}) async-start(f32[12,8,128]{2,1,0:T(8,128)} %shard_map.70), calls=%async_computation.2 | async-start | bytes 98304 | tf_op jit(solution)/shard_map/all_to_all | solution.py:153
  64.1 10.7 %collective-permute-start.4 = (bf16[3,8,112,128]{3,2,1,0:T(8,128)(2,1)S(1)}, bf16[3,8,112,128]{3,2,1,0:T(8,128)(2,1)S(1)}, u32[]{:S(2)}, u32[]{:S(2)}) collective-permute-start(bf16[3,8,112,128]{3,2,1,0:T(8,128)(2,1)S(1)} %pad_maximum_fusion.own_ref), channel_id=1, source_target_pairs={{0,1},{1,0},{2,3},{3,2},{4,5},{5,4},{6,7},{7,6},{8,9},{9,8},{10,11... | collective-permute-start | bytes 2064392 | tf_op jit(solution)/shard_map/ppermute | solution.py:150
